TPU v7x, 128 devices: a whole 4x4x4 slice. The times are simulated.
128 devices in a mesh: section: 32 (over y, x, core), tp: 4 (over z).
Axes of the slice: x: 4, y: 4, z: 4, core: 2. Of those that a mesh axis runs over, the one named last changes fastest.
Arguments:
- tokens: bfloat16 [512, 2048], P('tp'), may hold values from -6 to 6
- cotangent: bfloat16 [512, 2048], P('tp'), may hold values from -0.119628906 to 0.119628906
- value_weight: bfloat16 [32, 2048, 512], P('section', None, 'tp'), may hold values from -0.125 to 0.125
- output_weight: bfloat16 [32, 2048, 512], P('section', None, 'tp'), may hold values from -0.25 to 0.25
- value_first: float32 [32, 2048, 512], P('section', None, 'tp'), may hold values from -1.8 to 1.8
- output_first: float32 [32, 2048, 512], P('section', None, 'tp'), may hold values from -1.8 to 1.8
- value_second: float32 [32, 2048, 512], P('section', None, 'tp'), may hold values from 0.01 to 1
- output_second: float32 [32, 2048, 512], P('section', None, 'tp'), may hold values from 0.01 to 1
- layer_map: int32 [24], replicated, may hold values from 0 to 15, as said below
- old_section: int32 [16], replicated, may hold values from 0 to 31, as said below
- new_section: int32 [24], replicated, may hold values from 0 to 31, as said below
Outputs:
- new_value_weight: bfloat16 [32, 2048, 512], P('section', None, 'tp')
- new_output_weight: bfloat16 [32, 2048, 512], P('section', None, 'tp')
- new_value_first: float32 [32, 2048, 512], P('section', None, 'tp')
- new_output_first: float32 [32, 2048, 512], P('section', None, 'tp')
- new_value_second: float32 [32, 2048, 512], P('section', None, 'tp')
- new_output_second: float32 [32, 2048, 512], P('section', None, 'tp')
Inputs may be any that keep to these rules, and one draw needn't show every extreme that they name: `layer_map`: Non-decreasing; every old layer appears once or twice. `old_section`: strictly increasing. `new_section`: strictly increasing.
All inputs are finite; a program needn't handle non-finite values.
Results may differ from a plain program's by a relative error of at most 0.025.
Values may be sent and summed in bfloat16 or wider, within the bound.
A program may use at most 128 MiB of HBM per device.

v0:
```python
import jax
import jax.numpy as jnp
from jax import lax
from jax.sharding import PartitionSpec as P

epsilon = 1e-05
beta_one = 0.9
beta_two = 0.95
step_rate = 0.003
adam_floor = 1e-08


def passed_along(block, axis, distance):
    devices = range(lax.axis_size(axis))
    route = [(i - distance, i) for i in devices if i - distance in devices]
    return lax.ppermute(block, axis, route)


def side_by_side(arrays, axis, split_dim, concat_dim, along):
    both = jnp.concatenate(arrays, axis=along)
    filled, at, outs = (
        lax.all_to_all(both, axis, split_axis=split_dim, concat_axis=concat_dim, tiled=True),
        0,
        [],
    )
    for a in arrays:
        outs.append(lax.slice_in_dim(filled, at, at + a.shape[along], axis=along))
        at += a.shape[along]
    return tuple(outs)


def side_by_side_2(arrays, axis, dim, along):
    widths = [a.shape[along] for a in arrays]
    both = jnp.concatenate(arrays, axis=along)
    filled = lax.all_gather(both, axis, axis=dim, tiled=True)
    return tuple(jnp.split(filled, [sum(widths[:k]) for k in range(1, len(widths))], axis=along))


def normalize(stream):
    widened = stream.astype(jnp.float32)
    factor = lax.rsqrt(jnp.mean(widened * widened, axis=-1, keepdims=True) + epsilon)
    return (widened * factor, factor)


def forward_layer(stream, value_full, output_full):
    normed, factor = normalize(stream)
    hidden = normed.astype(jnp.bfloat16)
    preact = jnp.dot(hidden, value_full, preferred_element_type=jnp.float32)
    unit_values = jax.nn.silu(preact).astype(jnp.bfloat16)
    mixing = lax.dot_general(
        unit_values, output_full, (((1,), (1,)), ((), ())), preferred_element_type=jnp.float32
    )
    return ((stream.astype(jnp.float32) + mixing).astype(jnp.bfloat16), preact, unit_values)


def backward_layer(stream, preact, grad_out, value_full, output_full):
    grad_units = jnp.dot(grad_out, output_full, preferred_element_type=jnp.float32)
    gate_value = jax.nn.sigmoid(preact)
    grad_inner = (grad_units * gate_value * (1.0 + preact * (1.0 - gate_value))).astype(
        jnp.bfloat16
    )
    grad_hidden = lax.dot_general(
        grad_inner, value_full, (((1,), (1,)), ((), ())), preferred_element_type=jnp.float32
    )
    normed, factor = normalize(stream)
    grad_stream = factor * (
        grad_hidden - normed * jnp.mean(grad_hidden * normed, axis=-1, keepdims=True)
    )
    return ((grad_out.astype(jnp.float32) + grad_stream).astype(jnp.bfloat16), grad_inner)


def hand_over(values, offset):
    return passed_along(values, "section", offset)


def adam_update(weight, first, second, gradient):
    first_new = beta_one * first + (1.0 - beta_one) * gradient
    second_new = beta_two * second + (1.0 - beta_two) * gradient * gradient
    weight_new = (
        weight.astype(jnp.float32) - step_rate * first_new / (jnp.sqrt(second_new) + adam_floor)
    ).astype(jnp.bfloat16)
    return (weight_new[None], first_new[None], second_new[None])


def body(
    tokens,
    cotangent,
    value_weight,
    output_weight,
    value_first,
    output_first,
    value_second,
    output_second,
    layer_map,
    old_section,
    new_section,
):
    sections = lax.axis_size("section")
    myself = lax.axis_index("section")
    positions = lax.iota(jnp.int32, sections)
    owner_match = new_section[None, :] == positions[:, None]
    has_layer = jnp.any(owner_match, axis=1)
    new_index = jnp.sum(
        jnp.where(owner_match, lax.iota(jnp.int32, new_section.shape[0])[None, :], 0), axis=1
    )
    map_match = new_index[:, None] == lax.iota(jnp.int32, layer_map.shape[0])[None, :]
    old_index = jnp.sum(jnp.where(map_match, layer_map[None, :], 0), axis=1)
    section_match = old_index[:, None] == lax.iota(jnp.int32, old_section.shape[0])[None, :]
    source = jnp.sum(jnp.where(section_match, old_section[None, :], 0), axis=1)
    holds_layer = jnp.any((positions == myself) & has_layer)
    keep_mask = has_layer.astype(jnp.float32)[:, None, None]
    weight_pieces = (
        lax.all_to_all(value_weight, "section", split_axis=1, concat_axis=0, tiled=True),
        lax.all_to_all(output_weight, "section", split_axis=1, concat_axis=0, tiled=True),
    )
    moment_pieces = side_by_side(
        (value_first, output_first, value_second, output_second), "section", 1, 0, 2
    )
    weight_mask = keep_mask.astype(jnp.bfloat16)
    picked_weights = [jnp.take(portion, source, axis=0) * weight_mask for portion in weight_pieces]
    picked_moments = [jnp.take(portion, source, axis=0) * keep_mask for portion in moment_pieces]
    arrived_weights = side_by_side((picked_weights[0], picked_weights[1]), "section", 0, 1, 2)
    arrived_moments = (
        lax.all_to_all(picked_moments[0], "section", split_axis=0, concat_axis=1, tiled=True),
        lax.all_to_all(picked_moments[1], "section", split_axis=0, concat_axis=1, tiled=True),
        lax.all_to_all(picked_moments[2], "section", split_axis=0, concat_axis=1, tiled=True),
        lax.all_to_all(picked_moments[3], "section", split_axis=0, concat_axis=1, tiled=True),
    )
    value_local = arrived_weights[0][0]
    output_local = arrived_weights[1][0]
    first_value = arrived_moments[0][0]
    first_output = arrived_moments[1][0]
    second_value = arrived_moments[2][0]
    second_output = arrived_moments[3][0]
    value_full, output_full = side_by_side_2((value_local, output_local), "tp", 1, 0)
    row_count, feature_count = tokens.shape
    channel_count = value_full.shape[1]
    blocks = 4
    block_rows = row_count // blocks
    step_count = sections + blocks - 1
    token_blocks = tokens.reshape(blocks, block_rows, feature_count)
    grad_blocks = cotangent.reshape(blocks, block_rows, feature_count)

    def forward_step(step_index, loop_state):
        stream, saved_in, saved_pre, saved_units = loop_state
        entering = token_blocks[jnp.minimum(step_index, blocks - 1)]
        stream = jnp.where(myself == 0, entering, stream)
        block_slot = step_index - myself
        active = (block_slot >= 0) & (block_slot < blocks)
        block_place = jnp.clip(block_slot, 0, blocks - 1)
        result, preact, unit_values = forward_layer(stream, value_full, output_full)
        result = jnp.where(holds_layer, result, stream)
        saved_in = jnp.where(
            active, lax.dynamic_update_index_in_dim(saved_in, stream, block_place, 0), saved_in
        )
        saved_pre = jnp.where(
            active, lax.dynamic_update_index_in_dim(saved_pre, preact, block_place, 0), saved_pre
        )
        saved_units = jnp.where(
            active,
            lax.dynamic_update_index_in_dim(saved_units, unit_values, block_place, 0),
            saved_units,
        )
        return (hand_over(result, 1), saved_in, saved_pre, saved_units)

    forward_init = (
        token_blocks[0],
        jnp.zeros((blocks, block_rows, feature_count), jnp.bfloat16),
        jnp.zeros((blocks, block_rows, channel_count), jnp.float32),
        jnp.zeros((blocks, block_rows, channel_count), jnp.bfloat16),
    )
    stream_last, saved_in, saved_pre, saved_units = lax.fori_loop(
        0, step_count, forward_step, forward_init
    )

    def backward_step(step_index, loop_state):
        flowing, saved_grad, saved_inner = loop_state
        entering = grad_blocks[jnp.minimum(step_index, blocks - 1)]
        flowing = jnp.where(myself == sections - 1, entering, flowing)
        block_slot = step_index - (sections - 1 - myself)
        active = (block_slot >= 0) & (block_slot < blocks)
        block_place = jnp.clip(block_slot, 0, blocks - 1)
        stream_in = saved_in[block_place]
        preact = saved_pre[block_place]
        result, grad_inner = backward_layer(stream_in, preact, flowing, value_full, output_full)
        result = jnp.where(holds_layer, result, flowing)
        saved_grad = jnp.where(
            active, lax.dynamic_update_index_in_dim(saved_grad, flowing, block_place, 0), saved_grad
        )
        saved_inner = jnp.where(
            active,
            lax.dynamic_update_index_in_dim(saved_inner, grad_inner, block_place, 0),
            saved_inner,
        )
        return (hand_over(result, -1), saved_grad, saved_inner)

    backward_init = (
        grad_blocks[0],
        jnp.zeros((blocks, block_rows, feature_count), jnp.bfloat16),
        jnp.zeros((blocks, block_rows, channel_count), jnp.bfloat16),
    )
    flowing_last, saved_grad, saved_inner = lax.fori_loop(
        0, step_count, backward_step, backward_init
    )
    hidden_all = normalize(saved_in.reshape(row_count, feature_count))[0].astype(jnp.bfloat16)
    grad_value = lax.dot_general(
        hidden_all,
        saved_inner.reshape(row_count, channel_count),
        (((0,), (0,)), ((), ())),
        preferred_element_type=jnp.float32,
    )
    grad_output = lax.dot_general(
        saved_grad.reshape(row_count, feature_count),
        saved_units.reshape(row_count, channel_count),
        (((0,), (0,)), ((), ())),
        preferred_element_type=jnp.float32,
    )
    grad_value, grad_output = (
        lax.psum_scatter(
            grad_value.astype(jnp.bfloat16), "tp", scatter_dimension=1, tiled=True
        ).astype(jnp.float32),
        lax.psum_scatter(
            grad_output.astype(jnp.bfloat16), "tp", scatter_dimension=1, tiled=True
        ).astype(jnp.float32),
    )
    owned = holds_layer.astype(jnp.float32)
    grad_value = grad_value * owned
    grad_output = grad_output * owned
    value_new = adam_update(value_local, first_value, second_value, grad_value)
    output_new = adam_update(output_local, first_output, second_output, grad_output)
    return (value_new[0], output_new[0], value_new[1], output_new[1], value_new[2], output_new[2])


def solution(mesh):
    placed = (
        P("tp", None),
        P("tp", None),
        P("section", None, "tp"),
        P("section", None, "tp"),
        P("section", None, "tp"),
        P("section", None, "tp"),
        P("section", None, "tp"),
        P("section", None, "tp"),
        P(),
        P(),
        P(),
    )
    return jax.shard_map(
        body,
        mesh=mesh,
        in_specs=placed,
        out_specs=(
            P("section", None, "tp"),
            P("section", None, "tp"),
            P("section", None, "tp"),
            P("section", None, "tp"),
            P("section", None, "tp"),
            P("section", None, "tp"),
        ),
        check_vma=False,
    )
```

profile of v0, /device:TPU:1, one launch (start us, length us, event | category | flops | bytes accessed | tf_op | source)
XLA Modules:
  0.0 1166.9 jit_solution(12036485693579018802)
XLA Ops:
  9.5 11.5 reduce.1
  21.9 8.6 all-to-all-start
  30.6 8.1 copy.44
  38.7 11.5 reduce.2
  51.5 7.4 all-to-all-start.1
  60.3 10.1 all-to-all-done.1
  72.7 20.8 %all_to_all.84 = bf16[32,64,256]{2,1,0:T(8,128)(2,1)S(1)} all-to-all(bf16[32,64,256]{2,1,0:T(8,128)(2,1)S(1)} %pad_maximum_fusion.1), channel_id=1, replica_groups=mesh['section'=32,'tp'=4] {'section'}, dimensions={0} | all-to-all | bytes 2097152 | tf_op jit(solution)/shard_map/all_to_all | solution.py:22
  98.3 11.7 %copy.34 = f32[1,2048,512]{2,0,1:T(1,128)} copy(f32[1,2048,512]{2,1,0:T(8,128)S(1)} %pad_maximum_fusion) | data formatting | bytes 8388608 | tf_op jit(solution)/shard_map/concatenate | solution.py:20
  116.8 28.8 %all-gather.2.cloned.1.call-done = bf16[4096,512]{1,0:T(8,128)(2,1)} async-done(((bf16[4096,128]{1,0:T(8,128)(2,1)}), bf16[4096,512]{1,0:T(8,128)(2,1)}) %all-gather.2.cloned.1.call-update) | async-done | bytes 4194320 | tf_op jit(solution)/shard_map/all_gather | solution.py:35
  149.5 428.6 %while.39 = (s32[]{:T(128)}, bf16[32,2048]{1,0:T(8,128)(2,1)S(1)}, bf16[4,32,2048]{2,1,0:T(8,128)(2,1)S(1)}, f32[4,32,512]{2,1,0:T(8,128)S(1)}, bf16[4,32,512]{2...) while((s32[]{:T(128)}, bf16[32,2048]{1,0:T(8,128)(2,1)S(1)}, ...), condition=%wide.region_7.10_spmd, body=%wide.region_5.0_spmd.sunk | while | flops 135200800 | bytes 6292657 | solution.py:172
  310.1 6.5 collective-permute-start
  323.1 6.5 collective-permute-start
  336.0 6.5 collective-permute-start
  349.0 6.5 collective-permute-start
  362.0 6.5 collective-permute-start
  375.0 6.5 collective-permute-start
  439.9 6.5 collective-permute-start
  452.8 6.5 collective-permute-start
  465.8 6.5 collective-permute-start
  478.8 6.5 collective-permute-start
  491.8 6.5 collective-permute-start
  504.7 6.5 collective-permute-start
  556.7 6.5 collective-permute-start
  569.6 6.5 collective-permute-start
  579.1 440.2 %while.40 = (s32[]{:T(128)}, bf16[32,2048]{1,0:T(8,128)(2,1)S(1)}, bf16[4,32,2048]{2,1,0:T(8,128)(2,1)}, bf16[4,32,512]{2,1,0:T(8,128)(2,1)S(1)}, pred[]{:T(512)...) while((s32[]{:T(128)}, bf16[32,2048]{1,0:T(8,128)(2,1)S(1)}, ...), condition=%wide.region_12.15_spmd, body=%wide.region_9.14_spmd.sunk | while | flops 135561248 | bytes 15271899 | solution.py:202
  585.2 7.2 collective-permute-done.1
  610.8 7.2 collective-permute-done.1
  636.3 7.2 collective-permute-done.1
  661.9 7.2 collective-permute-done.1
  675.2 6.5 collective-permute-done.1
  725.2 6.5 collective-permute-done.1
  737.7 6.5 collective-permute-done.1
  750.2 6.5 collective-permute-done.1
  762.7 6.5 collective-permute-done.1
  800.2 6.5 collective-permute-done.1
  812.7 6.5 collective-permute-done.1
  825.2 6.5 collective-permute-done.1
  837.7 6.5 collective-permute-done.1
  875.2 6.5 collective-permute-done.1
  887.7 6.5 collective-permute-done.1
  900.3 6.5 collective-permute-done.1
  912.8 6.5 collective-permute-done.1
  962.8 6.5 collective-permute-done.1
  1036.6 30.9 %all-to-all-start.7 = ((f32[32,64,128]{2,1,0:T(8,128)}), f32[32,64,128]{2,1,0:T(8,128)S(1)}, u32[]{:S(2)}, u32[]{:S(2)}) async-start(f32[32,64,128]{2,1,0:T(8,128)} %get-tuple-element.562), calls=%async_computation.7 | async-start | bytes 2097152 | tf_op jit(solution)/shard_map/all_to_all | solution.py:127
  1073.7 11.1 all-to-all-done.7
  1084.8 21.0 %all_to_all.85 = f32[32,64,128]{2,1,0:T(8,128)} all-to-all(f32[32,64,128]{2,1,0:T(8,128)S(1)} %copy-done.4), channel_id=1, replica_groups=mesh['section'=32,'tp'=4] {'section'}, dimensions={0} | all-to-all | bytes 2097152 | tf_op jit(solution)/shard_map/all_to_all | solution.py:126
  1105.7 21.0 %all_to_all.86 = f32[32,64,128]{2,1,0:T(8,128)} all-to-all(f32[32,64,128]{2,1,0:T(8,128)S(1)} %copy-done.3), channel_id=1, replica_groups=mesh['section'=32,'tp'=4] {'section'}, dimensions={0} | all-to-all | bytes 2097152 | tf_op jit(solution)/shard_map/all_to_all | solution.py:125
  1134.6 14.3 %all-to-all-done.4 = f32[32,64,128]{2,1,0:T(8,128)} async-done(((f32[32,64,128]{2,1,0:T(8,128)}), f32[32,64,128]{2,1,0:T(8,128)}, u32[]{:S(2)}, u32[]{:S(2)}) %all-to-all-start.4) | async-done | bytes 1048608 | tf_op jit(solution)/shard_map/all_to_all | solution.py:124
  (723 shorter events, 722.5 us)
Async XLA Ops:
  21.9 29.5 %all-to-all-start = ((bf16[32,2,4096]{2,1,0:T(2,128)(2,1)}), bf16[32,2,4096]{2,1,0:T(2,128)(2,1)S(1)}, u32[]{:S(2)}, u32[]{:S(2)}) async-start(bf16[32,2,4096]{2,1,0:T(2,128)(2,1)} %reshape.209), calls=%async_computation | async-start | bytes 1048576 | tf_op jit(solution)/shard_map/all_to_all | solution.py:113
  51.5 18.9 %all-to-all-start.1 = ((bf16[32,2,4096]{2,1,0:T(2,128)(2,1)}), bf16[32,2,4096]{2,1,0:T(2,128)(2,1)S(1)}, u32[]{:S(2)}, u32[]{:S(2)}) async-start(bf16[32,2,4096]{2,1,0:T(2,128)(2,1)} %reshape.207), calls=%async_computation.1 | async-start | bytes 1048576 | tf_op jit(solution)/shard_map/all_to_all | solution.py:114
  58.9 86.7 %all-gather.2.cloned.1.call-start = ((), (), s32[]{:S(2)}) async-start(), calls=%async_computation.10 | async-start | bytes 5242880 | tf_op jit(solution)/shard_map/all_gather | solution.py:35
  110.0 912.6 %all-to-all-start.3 = ((f32[1,2048,512]{2,0,1:T(1,128)}), f32[1,2048,512]{2,0,1:T(1,128)}, u32[]{:S(2)}, u32[]{:S(2)}) async-start(f32[1,2048,512]{2,0,1:T(1,128)} %copy.34), calls=%async_computation.3 | async-start | bytes 8388608 | tf_op jit(solution)/shard_map/all_to_all | solution.py:22
  114.9 1036.4 %reduce-scatter.7.cloned.1.call-start = ((), (), s32[]{:S(2)}) async-start(), calls=%async_computation.11 | async-start | bytes 2621440
  154.1 9.2 collective-permute-start
  310.1 8.4 collective-permute-start
  323.1 8.4 collective-permute-start
  336.0 8.4 collective-permute-start
  349.0 8.4 collective-permute-start
  362.0 8.4 collective-permute-start
  375.0 8.4 collective-permute-start
  388.0 8.4 collective-permute-start
  400.9 8.4 collective-permute-start
  413.9 8.4 collective-permute-start
  426.9 8.4 collective-permute-start
  439.9 8.4 collective-permute-start
  452.8 8.4 collective-permute-start
  465.8 8.4 collective-permute-start
  478.8 8.4 collective-permute-start
  491.8 8.4 collective-permute-start
  504.7 8.4 collective-permute-start
  517.7 8.4 collective-permute-start
  530.7 8.4 collective-permute-start
  543.7 8.4 collective-permute-start
  556.7 8.4 collective-permute-start
  569.6 8.4 collective-permute-start
  583.2 9.1 collective-permute-start.1
  608.8 9.1 collective-permute-start.1
  634.4 9.1 collective-permute-start.1
  660.0 9.1 collective-permute-start.1
  673.2 8.4 collective-permute-start.1
  685.7 8.4 collective-permute-start.1
  698.2 8.4 collective-permute-start.1
  723.2 8.4 collective-permute-start.1
  735.8 8.4 collective-permute-start.1
  748.3 8.4 collective-permute-start.1
  760.8 8.4 collective-permute-start.1
  773.3 8.4 collective-permute-start.1
  798.3 8.4 collective-permute-start.1
  810.8 8.4 collective-permute-start.1
  823.3 8.4 collective-permute-start.1
  835.8 8.4 collective-permute-start.1
  848.3 8.4 collective-permute-start.1
  860.8 8.4 collective-permute-start.1
  1036.6 48.1 %all-to-all-start.7 = ((f32[32,64,128]{2,1,0:T(8,128)}), f32[32,64,128]{2,1,0:T(8,128)S(1)}, u32[]{:S(2)}, u32[]{:S(2)}) async-start(f32[32,64,128]{2,1,0:T(8,128)} %get-tuple-element.562), calls=%async_computation.7 | async-start | bytes 2097152 | tf_op jit(solution)/shard_map/all_to_all | solution.py:127
  1067.6 85.7 %reduce-scatter.9.cloned.1.call-start = ((), (), s32[]{:S(2)}) async-start(), calls=%async_computation.12 | async-start | bytes 2621440
  1126.7 22.1 %all-to-all-start.4 = ((f32[32,64,128]{2,1,0:T(8,128)}), f32[32,64,128]{2,1,0:T(8,128)}, u32[]{:S(2)}, u32[]{:S(2)}) async-start(f32[32,64,128]{2,1,0:T(8,128)} %get-tuple-element.564), calls=%async_computation.4 | async-start | bytes 2097152 | tf_op jit(solution)/shard_map/all_to_all | solution.py:124
  (79 other events, 498.5 us)
Sparse Core Ops, SparseCore 0:
  95.8 49.7 all-gather.1
  1022.7 55.3 reduce-scatter.6
  1080.7 29.4 reduce-scatter.8
where the time goes:
time: 1170 us
  waiting for transfers between devices  362 us (31%)
  starting transfers between devices  322 us (28%)
  other arithmetic  176 us (15%)
  matrix products  169 us (14%)
  blocking collectives  62.8 us (5%)
  local copies, waits for them, and re-layouts  57.4 us (5%)
  between operations  14.7 us (1%)
    ppermute x70, waiting for transfers between devices, passed_along(): return lax.ppermute(block, axis, route)  297 us
    ppermute x70, starting transfers between devices, passed_along(): return lax.ppermute(block, axis, route)  265 us
    dot_general x35, matrix products, forward_layer(): preact = jnp.dot(hidden, value_full, preferred_element_type=jnp.float32)  73.6 us
    select_n x35, other arithmetic, backward_step(): jnp.where(active, lax.dynamic_update_index_in_dim(saved_grad, flowing, bl...  64.1 us
    dot_general x35, matrix products, forward_layer(): lax.dot_general(unit_values, output_full, (((1,), (1,)), ((), ())), prefe...  47.3 us
    select_n x35, other arithmetic, forward_step(): jnp.where(active, lax.dynamic_update_index_in_dim(saved_in, stream, block...  33.6 us
    all_to_all x1, starting transfers between devices, body(): lax.all_to_all(picked_moments[3], 'section', split_axis=0, concat_axis=1,...  30.9 us
    unnamed x42, local copies, waits for them, and re-layouts  29.7 us
  transfers between devices with their start and end apart: 78, of which 74 were waited for; matrix products, arithmetic and copies ran while one was open for 32% of the time, Pallas kernels for 0%

commit v1 on v0

v1 whole, which is shorter than its diff:
```python
import jax
import jax.numpy as jnp
from jax import lax
from jax.experimental import pallas as pl
from jax.experimental.pallas import tpu as pltpu
from jax.sharding import PartitionSpec as P

epsilon = 1e-05
beta_one = 0.9
beta_two = 0.95
step_rate = 0.003
adam_floor = 1e-08
f32 = jnp.float32
bf16 = jnp.bfloat16
both = ("section", "tp")
rows = 8


def value_of(w):
    return jnp.concatenate([w[:, z, 0, 0].reshape(-1, w.shape[-1]) for z in range(w.shape[1])], axis=1)


def output_of(w):
    return jnp.concatenate([w[:, z, 0, 1].reshape(-1, w.shape[-1]) for z in range(w.shape[1])], axis=1)


def forward_kernel(map_ref, x_ref, w_ref, in_ref, hid_ref, pre_ref, unit_ref, state):
    @pl.when(pl.program_id(0) == 0)
    def _():
        state[...] = x_ref[...]

    x = state[...]
    in_ref[0] = x.astype(bf16)
    factor = lax.rsqrt(jnp.mean(x * x, axis=-1, keepdims=True) + epsilon)
    hidden = (x * factor).astype(bf16)
    hid_ref[0] = hidden
    w = w_ref[...]
    pre = jnp.dot(hidden, value_of(w), preferred_element_type=f32)
    pre_ref[0] = pre
    units = jax.nn.silu(pre).astype(bf16)
    unit_ref[0] = units
    mixing = lax.dot_general(units, output_of(w), (((1,), (1,)), ((), ())), preferred_element_type=f32)
    state[...] = (x + mixing).astype(bf16).astype(f32)


def backward_kernel(map_ref, g_ref, w_ref, in_ref, pre_ref, out_g_ref, out_z_ref, state):
    @pl.when(pl.program_id(0) == 0)
    def _():
        state[...] = g_ref[...]

    g = state[...]
    gb = g.astype(bf16)
    out_g_ref[0] = gb
    w = w_ref[...]
    gu = jnp.dot(gb, output_of(w), preferred_element_type=f32)
    pre = pre_ref[0]
    s = jax.nn.sigmoid(pre)
    gz = (gu * s * (1.0 + pre * (1.0 - s))).astype(bf16)
    out_z_ref[0] = gz
    gh = lax.dot_general(gz, value_of(w), (((1,), (1,)), ((), ())), preferred_element_type=f32)
    x = in_ref[0].astype(f32)
    factor = lax.rsqrt(jnp.mean(x * x, axis=-1, keepdims=True) + epsilon)
    n = x * factor
    gs = factor * (gh - n * jnp.mean(gh * n, axis=-1, keepdims=True))
    state[...] = (g + gs).astype(bf16).astype(f32)


def run_layers(kernel, layer_map, start, weights, extra, outs, backward):
    new = layer_map.shape[0]
    at = (lambda j: new - 1 - j) if backward else (lambda j: j)
    wshape = weights.shape

    def per_layer(a):
        return pl.BlockSpec((1,) + a.shape[1:], lambda j, m: (at(j), 0, 0))

    size = 2 * wshape[0] * wshape[1] * 2 * wshape[4] * wshape[5]
    return pl.pallas_call(
        kernel,
        grid_spec=pltpu.PrefetchScalarGridSpec(
            num_scalar_prefetch=1,
            grid=(new,),
            in_specs=[
                pl.BlockSpec(start.shape, lambda j, m: (0, 0)),
                pl.BlockSpec(
                    (wshape[0], wshape[1], 1) + wshape[3:], lambda j, m: (0, 0, m[at(j)], 0, 0, 0)
                ),
            ]
            + [per_layer(a) for a in extra],
            out_specs=[per_layer(a) for a in outs],
            scratch_shapes=[pltpu.VMEM(start.shape, f32)],
        ),
        out_shape=outs,
        compiler_params=pltpu.CompilerParams(
            dimension_semantics=("arbitrary",), vmem_limit_bytes=48 * 2**20
        ),
        cost_estimate=pl.CostEstimate(
            flops=new * 4 * rows * size // 4, bytes_accessed=new * size, transcendentals=0
        ),
    )(layer_map, start, weights, *extra)


def pick_kernel(index_ref, keep_ref, in_ref, out_ref):
    def one(k, carry):
        kept = in_ref[index_ref[k]] * keep_ref[k].astype(f32).astype(bf16)
        out_ref[k] = kept
        return carry

    lax.fori_loop(0, out_ref.shape[0], one, 0)


def pick_slots(index, keep, pieces):
    whole = pl.BlockSpec(memory_space=pltpu.VMEM)
    scalar = pl.BlockSpec(memory_space=pltpu.SMEM)
    flat = pieces.reshape(pieces.shape[0], -1, pieces.shape[-1])
    got = pl.pallas_call(
        pick_kernel,
        in_specs=[scalar, scalar, whole],
        out_specs=whole,
        out_shape=jax.ShapeDtypeStruct((index.shape[0],) + flat.shape[1:], bf16),
        compiler_params=pltpu.CompilerParams(vmem_limit_bytes=24 * 2**20),
    )(index, keep, flat)
    return got.reshape((index.shape[0],) + pieces.shape[1:])


def pick(onehot, pieces):
    flat = pieces.reshape(pieces.shape[0], -1, pieces.shape[-1])
    got = lax.dot_general(onehot, flat, (((1,), (0,)), ((), ())), preferred_element_type=bf16)
    return got.reshape((onehot.shape[0],) + pieces.shape[1:])


def adam_update(weight, first, second, gradient, owned):
    first_new = beta_one * first + (1.0 - beta_one) * gradient
    second_new = beta_two * second + (1.0 - beta_two) * gradient * gradient
    weight_new = weight - step_rate * first_new / (jnp.sqrt(second_new) + adam_floor)
    weight_new = jnp.where(owned, weight_new, 0.0).astype(bf16)
    return (weight_new[None], first_new[None], second_new[None])


def body(
    tokens,
    cotangent,
    value_weight,
    output_weight,
    value_first,
    output_first,
    value_second,
    output_second,
    layer_map,
    old_section,
    new_section,
):
    sections = lax.axis_size("section")
    width = lax.axis_size("tp")
    myself = lax.axis_index("section")
    column = lax.axis_index("tp")
    new = new_section.shape[0]
    features, channels = value_weight.shape[1:]
    part = features // sections
    positions = lax.iota(jnp.int32, sections)
    owner_match = positions[:, None] == new_section[None, :]
    map_match = layer_map[:, None] == lax.iota(jnp.int32, old_section.shape[0])[None, :]
    source = jnp.sum(jnp.where(map_match, old_section[None, :], 0), axis=1)
    holds = jnp.any(owner_match, axis=1)
    wanted = jnp.sum(jnp.where(owner_match, source[None, :], 0), axis=1)
    send_layer = owner_match.astype(bf16)
    owned = jnp.any(new_section == myself)
    my_layer = jnp.sum(jnp.where(new_section == myself, lax.iota(jnp.int32, new), 0))
    my_old = jnp.sum(jnp.where(lax.iota(jnp.int32, new) == my_layer, layer_map, 0))

    def pieces_of(arrays):
        return jnp.stack([a.reshape(sections, part, channels).astype(bf16) for a in arrays], axis=1)

    def spread(a):
        return lax.all_to_all(a, "section", split_axis=0, concat_axis=0, tiled=True)

    weight_pieces = pick_slots(
        old_section, jnp.ones_like(old_section), spread(pieces_of((value_weight, output_weight)))
    )
    gathered = lax.all_gather(weight_pieces, both)
    gathered = gathered.reshape((sections, width) + weight_pieces.shape)

    moments = pick_slots(
        wanted,
        holds.astype(jnp.int32),
        spread(pieces_of((value_first, output_first, value_second, output_second))),
    )
    moments = spread(moments)

    count = tokens.shape[0] // sections

    def mine(a):
        block = lax.dynamic_slice_in_dim(a, myself * count, count, axis=0).astype(f32)
        return jnp.pad(block, ((0, rows - count), (0, 0)))

    inner = width * channels
    shape = jax.ShapeDtypeStruct
    saved_in, hidden, pre, units = run_layers(
        forward_kernel,
        layer_map,
        mine(tokens),
        gathered,
        (),
        [
            shape((new, rows, features), bf16),
            shape((new, rows, features), bf16),
            shape((new, rows, inner), f32),
            shape((new, rows, inner), bf16),
        ],
        False,
    )
    grads, inner_grads = run_layers(
        backward_kernel,
        layer_map,
        mine(cotangent),
        gathered,
        (saved_in, pre),
        [shape((new, rows, features), bf16), shape((new, rows, inner), bf16)],
        True,
    )

    def to_owner(wide, narrow):
        w = pick(send_layer, wide[:, :count])
        n = pick(send_layer, narrow[:, :count])
        n = n.reshape(sections, count, width, channels).transpose(0, 2, 1, 3)
        w = jnp.broadcast_to(w[:, None], (sections, width, count, features))
        message = jnp.concatenate([w, n], axis=-1).reshape(sections * width, count, features + channels)
        got = lax.all_to_all(message, both, split_axis=0, concat_axis=0, tiled=True)
        got = got.reshape(sections * width * count, features + channels)
        return got[:, :features], got[:, features:]

    hidden_all, units_all = to_owner(hidden, units)
    grads_all, inner_all = to_owner(grads, inner_grads)

    def weight_grad(a, b):
        return lax.dot_general(a, b, (((0,), (0,)), ((), ())), preferred_element_type=f32)

    grad_value = weight_grad(hidden_all, inner_all)
    grad_output = weight_grad(grads_all, units_all)
    own = lax.dynamic_slice(
        gathered, (0, column, my_old, 0, 0, 0), (sections, 1, 1, 2, part, channels)
    )
    own = own.reshape(sections, 2, part, channels).astype(f32)
    moments = moments.astype(f32)

    def full(a):
        return a.reshape(features, channels)

    value_new = adam_update(full(own[:, 0]), full(moments[:, 0]), full(moments[:, 2]), grad_value, owned)
    output_new = adam_update(full(own[:, 1]), full(moments[:, 1]), full(moments[:, 3]), grad_output, owned)
    return (value_new[0], output_new[0], value_new[1], output_new[1], value_new[2], output_new[2])


def solution(mesh):
    split = P("section", None, "tp")
    placed = (P("tp", None),) * 2 + (split,) * 6 + (P(),) * 3
    return jax.shard_map(body, mesh=mesh, in_specs=placed, out_specs=(split,) * 6, check_vma=False)
```

time: 1170 us -> 426 us (0.36)
  starting transfers between devices: 322 us -> 20.8 us
  other arithmetic: 176 us -> 16.6 us
  matrix products: 169 us -> 11.9 us
  waiting for transfers between devices: 362 us -> 230 us
  Pallas kernels: 0 us -> 86.8 us
  local copies, waits for them, and re-layouts: 57.4 us -> 16.2 us
  blocking collectives: 62.8 us -> 25.7 us
    ppermute x70 -> x0, waiting for transfers between devices: 297 us -> none  [passed_along(): return lax.ppermute(block, axis, route)]
    ppermute x70 -> x0, starting transfers between devices: 265 us -> none  [passed_along(): return lax.ppermute(block, axis, route)]
    dot_general x142 -> x6, matrix products: 169 us -> 11.9 us  [the longest x2 9.92 us: weight_grad(): lax.dot_general(a, b, (((0,), (0,)), ((), ())), preferred_element_type=f32)]
    select_n x141 -> x0, other arithmetic: 126 us -> none  [the longest x35 64.1 us: backward_step(): jnp.where(active, lax.dynamic_update_index_in_dim(saved_grad, flowing, bl...]
    all_gather x1, waiting for transfers between devices: 28.8 us -> 154 us  [body(): gathered = lax.all_gather(weight_pieces, both)]
    pallas_call x0 -> x4, Pallas kernels: none -> 86.8 us  [the longest x2 82.7 us: run_layers(): pl.pallas_call(kernel, grid_spec=pltpu.PrefetchScalarGridSpec(num_scalar_...]
    all_to_all x5 -> x4, waiting for transfers between devices: 35.4 us -> 76 us  [the longest x2 43.1 us: to_owner(): got = lax.all_to_all(message, both, split_axis=0, concat_axis=0, tiled=True)]
    all_to_all x3 -> x1, blocking collectives: 62.8 us -> 25.7 us  [spread(): return lax.all_to_all(a, 'section', split_axis=0, concat_axis=0, tiled=True)]
  transfers between devices with their start and end apart: 78 -> 5, of which waited for: 74 -> 4; matrix products, arithmetic and copies ran while one was open for 32% -> 7% of each run, Pallas kernels for 0% -> 20%
where the time goes in v1:
time: 426 us; the launch traced here: 424 us
  waiting for transfers between devices  230 us (54%)
  Pallas kernels  86.8 us (20%)
  blocking collectives  25.7 us (6%)
  starting transfers between devices  20.8 us (5%)
  other arithmetic  16.6 us (4%)
  local copies, waits for them, and re-layouts  16.2 us (4%)
  between operations  16.2 us (4%)
  matrix products  11.9 us (3%)
    all_gather x1, waiting for transfers between devices, body(): gathered = lax.all_gather(weight_pieces, both)  154 us
    pallas_call x2, Pallas kernels, run_layers(): pl.pallas_call(kernel, grid_spec=pltpu.PrefetchScalarGridSpec(num_scalar_...  82.7 us
    all_to_all x2, waiting for transfers between devices, to_owner(): got = lax.all_to_all(message, both, split_axis=0, concat_axis=0, tiled=True)  43.1 us
    all_to_all x2, waiting for transfers between devices, spread(): return lax.all_to_all(a, 'section', split_axis=0, concat_axis=0, tiled=True)  32.9 us
    all_to_all x1, blocking collectives, spread(): return lax.all_to_all(a, 'section', split_axis=0, concat_axis=0, tiled=True)  25.7 us
    all_to_all x2, starting transfers between devices, to_owner(): got = lax.all_to_all(message, both, split_axis=0, concat_axis=0, tiled=True)  11.2 us
    dot_general x2, matrix products, weight_grad(): lax.dot_general(a, b, (((0,), (0,)), ((), ())), preferred_element_type=f32)  9.92 us
    all_to_all x2, starting transfers between devices, spread(): return lax.all_to_all(a, 'section', split_axis=0, concat_axis=0, tiled=True)  9.62 us
  transfers between devices with their start and end apart: 5, of which 4 were waited for; matrix products, arithmetic and copies ran while one was open for 7% of the time, Pallas kernels for 20%

profile of v1, /device:TPU:1, one launch (start us, length us, event | category | flops | bytes accessed | tf_op | source)
XLA Modules:
  0.0 424.4 jit_solution(11084339420288437185)
XLA Ops:
  7.2 1.3 pad_maximum_fusion.3
  8.5 25.7 %all_to_all.25 = bf16[32,2,64,128]{3,2,1,0:T(8,128)(2,1)S(1)} all-to-all(bf16[32,2,64,128]{3,2,1,0:T(8,128)(2,1)S(1)} %pad_maximum_fusion.3), channel_id=1, replica_groups=mesh['section'=32,'tp'=4] {'section'}, dimensions={0} | all-to-all | bytes 2097152 | tf_op jit(solution)/shard_map/all_to_all | solution.py:174
  34.2 1.6 shard_map.154
  35.9 0.1 convert_element_type.79
  36.0 1.0 copy-done.6
  37.1 0.3 copy-done.7
  37.4 1.6 pad_maximum_fusion.2
  39.0 4.2 all-to-all-start.1
  43.2 0.1 fusion.21
  43.3 0.1 select_reduce_fusion.1
  43.4 0.1 select_reduce_fusion.index_ref
  43.5 32.9 %all-to-all-done.1 = bf16[32,4,64,128]{3,2,1,0:T(8,128)(2,1)S(1)} async-done(((bf16[32,4,64,128]{3,2,1,0:T(8,128)(2,1)}), bf16[32,4,64,128]{3,2,1,0:T(8,128)(2,1)S(1)}, u32[]{:S(2)}, u32[]{:S(2)}) %all-to-all-start.1) | async-done | bytes 2097184 | tf_op jit(solution)/shard_map/all_to_all | solution.py:174
  76.4 2.5 shard_map.155
  78.9 5.4 %all-to-all-start.2 = ((bf16[32,4,64,128]{3,2,1,0:T(8,128)(2,1)}), bf16[32,4,64,128]{3,2,1,0:T(8,128)(2,1)S(1)}, u32[]{:S(2)}, u32[]{:S(2)}) async-start(bf16[32,4,64,128]{3,2,1,0:T(8,128)(2,1)} %bitcast.18), calls=%async_computation.2 | async-start | bytes 4194304 | tf_op jit(solution)/shard_map/all_to_all | solution.py:174
  84.3 0.8 constant_dynamic-slice_fusion
  85.2 154.1 %all-gather.2.cloned.1.call-done = bf16[128,16,2,64,128]{4,3,2,1,0:T(8,128)(2,1)} async-done(((bf16[1,16,2,64,128]{4,3,2,1,0:T(8,128)(2,1)}), bf16[128,16,2,64,128]{4,3,2,1,0:T(8,128)(2,1)}) %all-gather.2.cloned.1.call-update) | async-done | bytes 67108880 | tf_op jit(solution)/shard_map/all_gather | solution.py:179
  239.3 41.0 %shard_map.156 = (bf16[24,8,2048]{2,1,0:T(8,128)(2,1)S(1)}, bf16[24,8,2048]{2,1,0:T(8,128)(2,1)S(1)}, f32[24,8,512]{2,1,0:T(8,128)S(1)}, bf16[24,8,512]{2,1,0:T(8,128)(2,1)S(1)}) custom-call(s32[24]{0:T(128)S(1)} %copy-done, f32[8,2048]{1,0:T(8,128)S(1)} %pad_convert_fusion.1.x_ref, bf16[32,4,16,2,64,128]{5,4,3,2,1,0:T(8,128)(2,1)} %bitcast.6.w_ref), custom_call_target="tpu_custom_call" | custom-call | flops 805306368 | bytes 100663296 | tf_op jit(solution)/shard_map/pallas_call | solution.py:77
  280.3 41.8 %shard_map.157 = (bf16[24,8,2048]{2,1,0:T(8,128)(2,1)S(1)}, bf16[24,8,512]{2,1,0:T(8,128)(2,1)S(1)}) custom-call(s32[24]{0:T(128)S(1)} %copy-done, f32[8,2048]{1,0:T(8,128)S(1)} %pad_convert_fusion.g_ref, bf16[32,4,16,2,64,128]{5,4,3,2,1,0:T(8,128)(2,1)} %bitcast.6.w_ref, bf16[24,8,2048]{2,1,0:T(8,128)(2,1)S(1)} %get-tuple-element.14.in_ref, ...), custom_call_target="tpu_custom_call" | custom-call | flops 805306368 | bytes 100663296 | tf_op jit(solution)/shard_map/pallas_call | solution.py:77
  322.1 0.2 slice.47
  322.2 0.7 fusion.10
  323.0 1.2 copy.56
  324.2 0.3 fusion.16
  324.5 0.1 copy.58
  324.6 2.1 broadcast_in_dim.76
  326.7 2.5 pad_maximum_fusion.1
  329.3 1.4 copy-done.2
  330.6 7.4 %all-to-all-start.4 = ((bf16[128,4,2176]{2,1,0:T(4,128)(2,1)}), bf16[128,4,2176]{2,1,0:T(4,128)(2,1)}, u32[]{:S(2)}, u32[]{:S(2)}) async-start(bf16[128,4,2176]{2,1,0:T(4,128)(2,1)} %bitcast.24), calls=%async_computation.4 | async-start | bytes 4456448 | tf_op jit(solution)/shard_map/all_to_all | solution.py:227
  338.1 0.2 slice.44
  338.2 0.7 fusion.12
  339.0 0.4 copy.52
  339.4 0.3 fusion.18
  339.7 0.1 copy.54
  339.9 1.0 broadcast_in_dim.75
  340.9 2.5 pad_maximum_fusion
  343.4 26.3 %all-to-all-done.4 = bf16[128,4,2176]{2,1,0:T(4,128)(2,1)} async-done(((bf16[128,4,2176]{2,1,0:T(4,128)(2,1)}), bf16[128,4,2176]{2,1,0:T(4,128)(2,1)}, u32[]{:S(2)}, u32[]{:S(2)}) %all-to-all-start.4) | async-done | bytes 2228256 | tf_op jit(solution)/shard_map/all_to_all | solution.py:227
  369.7 3.8 all-to-all-start.3
  373.5 0.6 fusion.30
  374.1 1.3 fusion.31
  377.3 0.6 compare_reduce_fusion
  377.9 2.1 convert_element_type.87
  380.0 2.1 slice_multiply_fusion
  382.1 1.5 bitcast_convert_fusion
  383.6 1.1 fusion.34
  384.7 4.0 reshape.116
  388.7 16.8 %all-to-all-done.3 = bf16[128,4,2176]{2,1,0:T(4,128)(2,1)S(1)} async-done(((bf16[128,4,2176]{2,1,0:T(4,128)(2,1)}), bf16[128,4,2176]{2,1,0:T(4,128)(2,1)S(1)}, u32[]{:S(2)}, u32[]{:S(2)}) %all-to-all-start.3) | async-done | bytes 2228256 | tf_op jit(solution)/shard_map/all_to_all | solution.py:227
  405.6 2.1 reshape.113
  407.6 6.0 %fusion.7 = (bf16[2048,128]{1,0:T(8,128)(2,1)}, f32[2048,128]{1,0:T(8,128)}, f32[2048,128]{1,0:T(8,128)}) fusion(f32[32,1,64,128]{3,2,1,0:T(8,128)} %get-tuple-element.28, pred[]{:T(512)} %compare_reduce_fusion, f32[32,1,64,128]{3,2,1,0:T(8,128)} %get-tuple-element.25, f32[32,1,64,128]{3,2,1,0:T(8,128)} %get-tuple-element.24, ...), kind=kOutput, calls=%fused_computation.19 | convolution fusion | flops 271319040 | bytes 7995904 | tf_op jit(solution)/shard_map/dot_general | solution.py:235
  413.7 3.9 fusion.9
  (33 shorter events, 0.4 us)
Async XLA Ops:
  7.2 27.1 %copy-start.1 = (s32[16]{0:T(128)S(1)}, s32[16]{0:T(128)}, u32[]{:S(2)}) copy-start(s32[16]{0:T(128)} %index_ref.1) | copy-start | bytes 196
  7.2 232.2 %all-gather.2.cloned.1.call-start = ((), (), s32[]{:S(2)}) async-start(), calls=%async_computation.5 | async-start | bytes 67633152 | tf_op jit(solution)/shard_map/all_gather | solution.py:179
  8.5 27.3 %copy-start.4 = (f32[1,2048,128]{2,1,0:T(8,128)S(1)}, f32[1,2048,128]{2,1,0:T(8,128)}, u32[]{:S(2)}) copy-start(f32[1,2048,128]{2,1,0:T(8,128)} %param.15) | copy-start | bytes 3145732
  34.2 1.7 copy-start.5
  35.8 1.2 copy-start.6
  35.9 1.5 copy-start.7
  39.0 4.2 copy-start.10
  39.0 4.3 %copy-start = (s32[24]{0:T(128)S(1)}, s32[24]{0:T(128)}, u32[]{:S(2)}) copy-start(s32[24]{0:T(128)} %map_ref.3) | copy-start | bytes 292
  39.0 37.4 %all-to-all-start.1 = ((bf16[32,4,64,128]{3,2,1,0:T(8,128)(2,1)}), bf16[32,4,64,128]{3,2,1,0:T(8,128)(2,1)S(1)}, u32[]{:S(2)}, u32[]{:S(2)}) async-start(bf16[32,4,64,128]{3,2,1,0:T(8,128)(2,1)} %pad_maximum_fusion.2), calls=%async_computation.1 | async-start | bytes 4194304 | tf_op jit(solution)/shard_map/all_to_all | solution.py:174
  78.9 250.4 %all-to-all-start.2 = ((bf16[32,4,64,128]{3,2,1,0:T(8,128)(2,1)}), bf16[32,4,64,128]{3,2,1,0:T(8,128)(2,1)S(1)}, u32[]{:S(2)}, u32[]{:S(2)}) async-start(bf16[32,4,64,128]{3,2,1,0:T(8,128)(2,1)} %bitcast.18), calls=%async_computation.2 | async-start | bytes 4194304 | tf_op jit(solution)/shard_map/all_to_all | solution.py:174
  329.3 1.4 copy-start.2
  330.6 39.1 %all-to-all-start.4 = ((bf16[128,4,2176]{2,1,0:T(4,128)(2,1)}), bf16[128,4,2176]{2,1,0:T(4,128)(2,1)}, u32[]{:S(2)}, u32[]{:S(2)}) async-start(bf16[128,4,2176]{2,1,0:T(4,128)(2,1)} %bitcast.24), calls=%async_computation.4 | async-start | bytes 4456448 | tf_op jit(solution)/shard_map/all_to_all | solution.py:227
  369.7 35.9 %all-to-all-start.3 = ((bf16[128,4,2176]{2,1,0:T(4,128)(2,1)}), bf16[128,4,2176]{2,1,0:T(4,128)(2,1)S(1)}, u32[]{:S(2)}, u32[]{:S(2)}) async-start(bf16[128,4,2176]{2,1,0:T(4,128)(2,1)} %bitcast.22), calls=%async_computation.3 | async-start | bytes 4456448 | tf_op jit(solution)/shard_map/all_to_all | solution.py:227
  407.6 6.1 %copy-start.3 = (bf16[512,2176]{1,0:T(8,128)(2,1)S(1)}, bf16[512,2176]{1,0:T(8,128)(2,1)}, u32[]{:S(2)}) copy-start(bf16[512,2176]{1,0:T(8,128)(2,1)} %reshape.113) | copy-start | bytes 6684676
  407.6 6.1 %copy-start.8 = (f32[32,1,64,128]{3,2,1,0:T(8,128)S(1)}, f32[32,1,64,128]{3,2,1,0:T(8,128)}, u32[]{:S(2)}) copy-start(f32[32,1,64,128]{3,2,1,0:T(8,128)} %get-tuple-element.26) | copy-start | bytes 3145732
  407.6 6.1 %copy-start.9 = (f32[32,1,64,128]{3,2,1,0:T(8,128)S(1)}, f32[32,1,64,128]{3,2,1,0:T(8,128)}, u32[]{:S(2)}) copy-start(f32[32,1,64,128]{3,2,1,0:T(8,128)} %get-tuple-element.27) | copy-start | bytes 3145732
Sparse Core Ops, SparseCore 0:
  36.0 203.3 all-gather.1

commit v2 on v1

--- a/solution.py
+++ b/solution.py
@@ -3,6 +3,7 @@
 from jax import lax
 from jax.experimental import pallas as pl
 from jax.experimental.pallas import tpu as pltpu
+from jax.sharding import Mesh
 from jax.sharding import PartitionSpec as P
 
 epsilon = 1e-05
@@ -12,19 +13,154 @@
 adam_floor = 1e-08
 f32 = jnp.float32
 bf16 = jnp.bfloat16
-both = ("section", "tp")
+section = ("y", "x", "c")
+both = ("y", "x", "c", "z")
+orders = (("x", "y", "z"), ("y", "z", "x"), ("z", "x", "y"))
+ring = 4
+groups = 3
+chunk = 3
 rows = 8
-
-
-def value_of(w):
-    return jnp.concatenate([w[:, z, 0, 0].reshape(-1, w.shape[-1]) for z in range(w.shape[1])], axis=1)
-
-
-def output_of(w):
-    return jnp.concatenate([w[:, z, 0, 1].reshape(-1, w.shape[-1]) for z in range(w.shape[1])], axis=1)
-
-
-def forward_kernel(map_ref, x_ref, w_ref, in_ref, hid_ref, pre_ref, unit_ref, state):
+MESH = pl.DeviceIdType.MESH
+
+
+def unit_counts(units):
+    return [(units - g + groups - 1) // groups for g in range(groups)]
+
+
+def gather_kernel(counts, own_ref, out_ref, send, recv, own_sem):
+    me = {a: lax.axis_index(a) for a in both}
+
+    def beside(axis, step):
+        size = 2 if axis == "c" else ring
+        return {axis: lax.rem(me[axis] + step + size, size)}
+
+    barrier = pltpu.get_barrier_semaphore()
+    partners = [beside(a, s) for a in ("x", "y", "z") for s in (1, -1)] + [beside("c", 1)]
+    for p in partners:
+        pl.semaphore_signal(barrier, inc=1, device_id=p, device_id_type=MESH)
+    pl.semaphore_wait(barrier, len(partners))
+
+    used = [0]
+    started = []
+
+    def push(src, dst, to):
+        n = used[0]
+        used[0] += 1
+        copy = pltpu.make_async_remote_copy(
+            src_ref=src,
+            dst_ref=dst,
+            send_sem=send.at[n],
+            recv_sem=recv.at[n],
+            device_id=to,
+            device_id_type=MESH,
+        )
+        copy.start()
+        started.append(copy)
+        return copy
+
+    def place(g, phase, lo, size, at, half):
+        full = list(orders[g][:phase])
+        axis = orders[g][phase]
+        index = {a: pl.ds(me[a], 1) for a in ("x", "y", "z")}
+        for a in full:
+            index[a] = pl.ds(0, ring)
+        index[axis] = pl.ds(at, 1)
+        if half is not None:
+            if full:
+                index[full[0]] = pl.ds(half * (ring // 2), ring // 2)
+            else:
+                cut = size // 2
+                lo, size = (lo, cut) if half == 0 else (lo + cut, size - cut)
+        return out_ref.at[g, pl.ds(lo, size), me["c"], index["x"], index["y"], index["z"]]
+
+    def first(g, phase, lo, size):
+        axis = orders[g][phase]
+        here = place(g, phase, lo, size, me[axis], None)
+        return [push(here, here, beside(axis, s)) for s in (1, -1)]
+
+    def second(g, phase, lo, size, copies):
+        axis = orders[g][phase]
+        for c in copies:
+            c.wait_recv()
+        out = []
+        for half, s in ((0, 1), (1, -1)):
+            at = lax.rem(me[axis] - s + ring, ring)
+            part = place(g, phase, lo, size, at, half)
+            out.append(push(part, part, beside(axis, s)))
+        return out
+
+    mine = pltpu.make_async_copy(
+        own_ref, out_ref.at[:, :, me["c"], me["x"], me["y"], me["z"]], own_sem
+    )
+    mine.start()
+    mine.wait()
+    for phase in range(2):
+        copies = [first(g, phase, 0, counts[g]) for g in range(groups)]
+        copies = [second(g, phase, 0, counts[g], copies[g]) for g in range(groups)]
+        for pair in copies:
+            for c in pair:
+                c.wait_recv()
+    spans = [[(lo, min(chunk, n - lo)) for lo in range(0, n, chunk)] for n in counts]
+    total = max(len(x) for x in spans)
+    sent, halves, crossing = {}, {}, []
+
+    def begin(j):
+        for g in range(groups):
+            if j < len(spans[g]):
+                sent[g, j] = first(g, 2, *spans[g][j])
+
+    def cross(j):
+        for g in range(groups):
+            if (g, j) in halves:
+                for c in halves[g, j]:
+                    c.wait_recv()
+                lo, size = spans[g][j]
+                block = out_ref.at[g, pl.ds(lo, size), me["c"]]
+                crossing.append(push(block, block, beside("c", 1)))
+
+    begin(0)
+    begin(1)
+    for j in range(total):
+        for g in range(groups):
+            if (g, j) in sent:
+                halves[g, j] = second(g, 2, *spans[g][j], sent[g, j])
+        begin(j + 2)
+        if j:
+            cross(j - 1)
+    cross(total - 1)
+    for c in crossing:
+        c.wait_recv()
+    for c in started:
+        c.wait_send()
+
+
+def gather(own, units):
+    counts = unit_counts(units)
+    copies = sum(8 + 5 * -(-n // chunk) for n in counts)
+    part, channels = own.shape[-2:]
+    return pl.pallas_call(
+        lambda *refs: gather_kernel(counts, *refs),
+        in_specs=[pl.BlockSpec(memory_space=pl.ANY)],
+        out_specs=pl.BlockSpec(memory_space=pl.ANY),
+        out_shape=jax.ShapeDtypeStruct(own.shape[:2] + (2, ring, ring, ring, part, channels), bf16),
+        scratch_shapes=[
+            pltpu.SemaphoreType.DMA((copies,)),
+            pltpu.SemaphoreType.DMA((copies,)),
+            pltpu.SemaphoreType.DMA,
+        ],
+        compiler_params=pltpu.CompilerParams(
+            collective_id=0, has_side_effects=True, vmem_limit_bytes=16 * 2**20
+        ),
+        cost_estimate=pl.CostEstimate(flops=0, bytes_accessed=400 * 2**20, transcendentals=0),
+    )(own)
+
+
+def wide(w):
+    w = w[0, 0]
+    return jnp.concatenate([w[:, z].reshape(-1, w.shape[-1]) for z in range(w.shape[1])], axis=1)
+
+
+def forward_kernel(map_ref, x_ref, v_ref, o_ref, in_ref, hid_ref, pre_ref, unit_ref, state):
     @pl.when(pl.program_id(0) == 0)
     def _():
         state[...] = x_ref[...]
@@ -34,16 +170,15 @@
     factor = lax.rsqrt(jnp.mean(x * x, axis=-1, keepdims=True) + epsilon)
     hidden = (x * factor).astype(bf16)
     hid_ref[0] = hidden
-    w = w_ref[...]
-    pre = jnp.dot(hidden, value_of(w), preferred_element_type=f32)
+    pre = jnp.dot(hidden, wide(v_ref[...]), preferred_element_type=f32)
     pre_ref[0] = pre
     units = jax.nn.silu(pre).astype(bf16)
     unit_ref[0] = units
-    mixing = lax.dot_general(units, output_of(w), (((1,), (1,)), ((), ())), preferred_element_type=f32)
+    mixing = lax.dot_general(units, wide(o_ref[...]), (((1,), (1,)), ((), ())), preferred_element_type=f32)
     state[...] = (x + mixing).astype(bf16).astype(f32)
 
 
-def backward_kernel(map_ref, g_ref, w_ref, in_ref, pre_ref, out_g_ref, out_z_ref, state):
+def backward_kernel(map_ref, g_ref, v_ref, o_ref, in_ref, pre_ref, out_g_ref, out_z_ref, state):
     @pl.when(pl.program_id(0) == 0)
     def _():
         state[...] = g_ref[...]
@@ -51,13 +186,12 @@
     g = state[...]
     gb = g.astype(bf16)
     out_g_ref[0] = gb
-    w = w_ref[...]
-    gu = jnp.dot(gb, output_of(w), preferred_element_type=f32)
+    gu = jnp.dot(gb, wide(o_ref[...]), preferred_element_type=f32)
     pre = pre_ref[0]
     s = jax.nn.sigmoid(pre)
     gz = (gu * s * (1.0 + pre * (1.0 - s))).astype(bf16)
     out_z_ref[0] = gz
-    gh = lax.dot_general(gz, value_of(w), (((1,), (1,)), ((), ())), preferred_element_type=f32)
+    gh = lax.dot_general(gz, wide(v_ref[...]), (((1,), (1,)), ((), ())), preferred_element_type=f32)
     x = in_ref[0].astype(f32)
     factor = lax.rsqrt(jnp.mean(x * x, axis=-1, keepdims=True) + epsilon)
     n = x * factor
@@ -73,7 +207,14 @@
     def per_layer(a):
         return pl.BlockSpec((1,) + a.shape[1:], lambda j, m: (at(j), 0, 0))
 
-    size = 2 * wshape[0] * wshape[1] * 2 * wshape[4] * wshape[5]
+    def half(which):
+        def index(j, m):
+            unit = 2 * m[at(j)] + which
+            return (lax.rem(unit, groups), lax.div(unit, groups), 0, 0, 0, 0)
+
+        return pl.BlockSpec((1, 1) + wshape[2:], index)
+
+    size = 4 * wshape[2] * wshape[3] * wshape[4] * wshape[5]
     return pl.pallas_call(
         kernel,
         grid_spec=pltpu.PrefetchScalarGridSpec(
@@ -81,9 +222,8 @@
             grid=(new,),
             in_specs=[
                 pl.BlockSpec(start.shape, lambda j, m: (0, 0)),
-                pl.BlockSpec(
-                    (wshape[0], wshape[1], 1) + wshape[3:], lambda j, m: (0, 0, m[at(j)], 0, 0, 0)
-                ),
+                half(0),
+                half(1),
             ]
             + [per_layer(a) for a in extra],
             out_specs=[per_layer(a) for a in outs],
@@ -96,7 +236,7 @@
         cost_estimate=pl.CostEstimate(
             flops=new * 4 * rows * size // 4, bytes_accessed=new * size, transcendentals=0
         ),
-    )(layer_map, start, weights, *extra)
+    )(layer_map, start, weights, weights, *extra)
 
 
 def pick_kernel(index_ref, keep_ref, in_ref, out_ref):
@@ -149,10 +289,10 @@
     old_section,
     new_section,
 ):
-    sections = lax.axis_size("section")
-    width = lax.axis_size("tp")
-    myself = lax.axis_index("section")
-    column = lax.axis_index("tp")
+    sections = lax.axis_size(section)
+    width = lax.axis_size("z")
+    myself = lax.axis_index(section)
+    column = lax.axis_index("z")
     new = new_section.shape[0]
     features, channels = value_weight.shape[1:]
     part = features // sections
@@ -171,13 +311,22 @@
         return jnp.stack([a.reshape(sections, part, channels).astype(bf16) for a in arrays], axis=1)
 
     def spread(a):
-        return lax.all_to_all(a, "section", split_axis=0, concat_axis=0, tiled=True)
-
-    weight_pieces = pick_slots(
-        old_section, jnp.ones_like(old_section), spread(pieces_of((value_weight, output_weight)))
-    )
-    gathered = lax.all_gather(weight_pieces, both)
-    gathered = gathered.reshape((sections, width) + weight_pieces.shape)
+        return lax.all_to_all(a, section, split_axis=0, concat_axis=0, tiled=True)
+
+    def turned(a):
+        return a.reshape(2, ring, ring, part * channels).transpose(2, 1, 0, 3)
+
+    old = old_section.shape[0]
+    pieces = spread(pieces_of((turned(value_weight), turned(output_weight))))
+    deep = unit_counts(2 * old)[0]
+    unit = jnp.minimum(
+        groups * lax.iota(jnp.int32, deep)[None, :] + lax.iota(jnp.int32, groups)[:, None], 2 * old - 1
+    ).reshape(-1)
+    unit_match = (unit // 2)[:, None] == lax.iota(jnp.int32, old)[None, :]
+    slots = 2 * jnp.sum(jnp.where(unit_match, old_section[None, :], 0), axis=1) + unit % 2
+    own = pick_slots(slots, jnp.ones_like(slots), pieces.reshape(2 * sections, part, channels))
+    gathered = gather(own.reshape(groups, deep, part, channels), 2 * old)
+    gathered = gathered.reshape(groups, deep, sections, width, part, channels)
 
     moments = pick_slots(
         wanted,
@@ -236,21 +385,27 @@
 
     grad_value = weight_grad(hidden_all, inner_all)
     grad_output = weight_grad(grads_all, units_all)
-    own = lax.dynamic_slice(
-        gathered, (0, column, my_old, 0, 0, 0), (sections, 1, 1, 2, part, channels)
-    )
-    own = own.reshape(sections, 2, part, channels).astype(f32)
+    def own_of(which):
+        unit = 2 * my_old + which
+        got = lax.dynamic_slice(
+            gathered,
+            (unit % groups, unit // groups, 0, column, 0, 0),
+            (1, 1, sections, 1, part, channels),
+        )
+        return got.reshape(features, channels).astype(f32)
+
     moments = moments.astype(f32)
 
     def full(a):
         return a.reshape(features, channels)
 
-    value_new = adam_update(full(own[:, 0]), full(moments[:, 0]), full(moments[:, 2]), grad_value, owned)
-    output_new = adam_update(full(own[:, 1]), full(moments[:, 1]), full(moments[:, 3]), grad_output, owned)
+    value_new = adam_update(own_of(0), full(moments[:, 0]), full(moments[:, 2]), grad_value, owned)
+    output_new = adam_update(own_of(1), full(moments[:, 1]), full(moments[:, 3]), grad_output, owned)
     return (value_new[0], output_new[0], value_new[1], output_new[1], value_new[2], output_new[2])
 
 
 def solution(mesh):
-    split = P("section", None, "tp")
-    placed = (P("tp", None),) * 2 + (split,) * 6 + (P(),) * 3
-    return jax.shard_map(body, mesh=mesh, in_specs=placed, out_specs=(split,) * 6, check_vma=False)
+    split = P(section, None, "z")
+    placed = (P("z", None),) * 2 + (split,) * 6 + (P(),) * 3
+    fine = Mesh(mesh.devices.reshape(ring, ring, 2, ring), both)
+    return jax.shard_map(body, mesh=fine, in_specs=placed, out_specs=(split,) * 6, check_vma=False)

time: 426 us -> 422 us (level)
  Pallas kernels: 86.8 us -> 263 us
  waiting for transfers between devices: 230 us -> 83.4 us
  blocking collectives: 25.7 us -> 0 us
  between operations: 16.2 us -> 1.74 us
  starting transfers between devices: 20.8 us -> 28.4 us
    pallas_call x0 -> x1, Pallas kernels: none -> 177 us  [gather(): pl.pallas_call(lambda *refs: gather_kernel(counts, *refs), in_specs=[pl.B...]
    all_gather x1 -> x0, waiting for transfers between devices: 154 us -> none  [body(): gathered = lax.all_gather(weight_pieces, both)]
    all_to_all x1 -> x0, blocking collectives: 25.7 us -> none  [spread(): return lax.all_to_all(a, 'section', split_axis=0, concat_axis=0, tiled=True)]
    all_to_all x2, waiting for transfers between devices: 43.1 us -> 55.3 us  [to_owner(): got = lax.all_to_all(message, both, split_axis=0, concat_axis=0, tiled=True)]
    all_to_all x2 -> x3, starting transfers between devices: 9.62 us -> 16.7 us  [spread(): return lax.all_to_all(a, section, split_axis=0, concat_axis=0, tiled=True)]
    all_to_all x2 -> x3, waiting for transfers between devices: 32.9 us -> 28.1 us  [spread(): return lax.all_to_all(a, section, split_axis=0, concat_axis=0, tiled=True)]
  transfers between devices with their start and end apart: 5 -> 5, of which waited for: 4 -> 4; matrix products, arithmetic and copies ran while one was open for 7% -> 7% of each run, Pallas kernels for 20% -> 63%
where the time goes in v2:
time: 422 us; the launch traced here: 420 us
  Pallas kernels  263 us (62%)
  waiting for transfers between devices  83.4 us (20%)
  starting transfers between devices  28.4 us (7%)
  local copies, waits for them, and re-layouts  20.2 us (5%)
  other arithmetic  14.8 us (4%)
  matrix products  7.97 us (2%)
    pallas_call x1, Pallas kernels, gather(): pl.pallas_call(lambda *refs: gather_kernel(counts, *refs), in_specs=[pl.B...  177 us
    pallas_call x2, Pallas kernels, run_layers(): pl.pallas_call(kernel, grid_spec=pltpu.PrefetchScalarGridSpec(num_scalar_...  82.6 us
    all_to_all x2, waiting for transfers between devices, to_owner(): got = lax.all_to_all(message, both, split_axis=0, concat_axis=0, tiled=True)  55.3 us
    all_to_all x3, waiting for transfers between devices, spread(): return lax.all_to_all(a, section, split_axis=0, concat_axis=0, tiled=True)  28.1 us
    all_to_all x3, starting transfers between devices, spread(): return lax.all_to_all(a, section, split_axis=0, concat_axis=0, tiled=True)  16.7 us
    all_to_all x2, starting transfers between devices, to_owner(): got = lax.all_to_all(message, both, split_axis=0, concat_axis=0, tiled=True)  11.7 us
  transfers between devices with their start and end apart: 5, of which 4 were waited for; matrix products, arithmetic and copies ran while one was open for 7% of the time, Pallas kernels for 63%

profile of v2, /device:TPU:1, one launch (start us, length us, event | category | flops | bytes accessed | tf_op | source)
XLA Modules:
  0.0 419.9 jit_solution(5809907138239288685)
XLA Ops:
  0.6 1.2 reshape.155
  1.9 0.5 copy.31
  2.4 0.4 stack_reshape.6
  3.0 0.5 copy.32
  3.5 0.4 stack_reshape.7
  3.9 1.1 pad_maximum_fusion.3
  5.0 8.7 %all-to-all-start = ((bf16[32,2,64,128]{3,2,1,0:T(8,128)(2,1)}), bf16[32,2,64,128]{3,2,1,0:T(8,128)(2,1)S(1)}, u32[]{:S(2)}, u32[]{:S(2)}) async-start(bf16[32,2,64,128]{3,2,1,0:T(8,128)(2,1)} %pad_maximum_fusion.3), calls=%async_computation | async-start | bytes 2097152 | tf_op jit(solution)/shard_map/all_to_all | solution.py:314
  13.9 1.4 convert_element_type.91
  15.3 1.3 convert_element_type.85
  16.6 1.6 pad_maximum_fusion.2
  18.2 12.7 %all-to-all-done = bf16[32,2,64,128]{3,2,1,0:T(8,128)(2,1)S(1)} async-done(((bf16[32,2,64,128]{3,2,1,0:T(8,128)(2,1)}), bf16[32,2,64,128]{3,2,1,0:T(8,128)(2,1)S(1)}, u32[]{:S(2)}, u32[]{:S(2)}) %all-to-all-start) | async-done | bytes 1048608 | tf_op jit(solution)/shard_map/all_to_all | solution.py:314
  30.9 4.1 all-to-all-start.1
  35.1 0.8 constant_dynamic-slice_fusion
  35.9 1.0 shard_map.154
  36.9 177.3 %shard_map.155 = bf16[3,11,2,4,4,4,64,128]{7,6,5,4,3,2,1,0:T(8,128)(2,1)} custom-call(bf16[3,11,64,128]{3,2,1,0:T(8,128)(2,1)S(1)} %bitcast.59), custom_call_target="tpu_custom_call" | custom-call | bytes 419430400 | tf_op jit(solution)/shard_map/pallas_call | solution.py:141
  214.2 41.5 %shard_map.157 = (bf16[24,8,2048]{2,1,0:T(8,128)(2,1)S(1)}, bf16[24,8,2048]{2,1,0:T(8,128)(2,1)S(1)}, f32[24,8,512]{2,1,0:T(8,128)S(1)}, bf16[24,8,512]{2,1,0:T(8,128)(2,1)S(1)}) custom-call(s32[24]{0:T(128)S(1)} %copy-done, f32[8,2048]{1,0:T(8,128)S(1)} %pad_convert_fusion.1.x_ref, bf16[3,11,32,4,64,128]{5,4,3,2,1,0:T(8,128)(2,1)} %bitcast.4.v_ref.o_ref, ...), custom_call_target="tpu_custom_call" | custom-call | flops 805306368 | bytes 100663296 | tf_op jit(solution)/shard_map/pallas_call | solution.py:218
  255.7 41.1 %shard_map.158 = (bf16[24,8,2048]{2,1,0:T(8,128)(2,1)S(1)}, bf16[24,8,512]{2,1,0:T(8,128)(2,1)S(1)}) custom-call(s32[24]{0:T(128)S(1)} %copy-done, f32[8,2048]{1,0:T(8,128)S(1)} %pad_convert_fusion.g_ref, bf16[3,11,32,4,64,128]{5,4,3,2,1,0:T(8,128)(2,1)} %bitcast.4.v_ref.o_ref, bf16[3,11,32,4,64,128]{5,4,3,2,1,0:T(8,128)(2,1)} %bitcast.4.v_ref.o_ref, ...), custom_call_target="tpu_custom_call" | custom-call | flops 805306368 | bytes 100663296 | tf_op jit(solution)/shard_map/pallas_call | solution.py:218
  296.9 0.2 slice.40
  297.0 0.7 fusion.10
  297.8 1.2 copy.42
  299.0 0.3 fusion.16
  299.5 2.1 broadcast_in_dim.96
  301.6 2.5 pad_maximum_fusion.1
  304.1 6.9 %all-to-all-start.4 = ((bf16[128,4,2176]{2,1,0:T(4,128)(2,1)}), bf16[128,4,2176]{2,1,0:T(4,128)(2,1)}, u32[]{:S(2)}, u32[]{:S(2)}) async-start(bf16[128,4,2176]{2,1,0:T(4,128)(2,1)} %bitcast.60), calls=%async_computation.4 | async-start | bytes 4456448 | tf_op jit(solution)/shard_map/all_to_all | solution.py:376
  311.0 0.2 slice.37
  311.2 0.7 fusion.12
  311.9 0.4 copy.38
  312.4 0.3 fusion.18
  312.8 1.0 broadcast_in_dim.95
  313.9 2.5 pad_maximum_fusion
  316.4 26.3 %all-to-all-done.4 = bf16[128,4,2176]{2,1,0:T(4,128)(2,1)} async-done(((bf16[128,4,2176]{2,1,0:T(4,128)(2,1)}), bf16[128,4,2176]{2,1,0:T(4,128)(2,1)}, u32[]{:S(2)}, u32[]{:S(2)}) %all-to-all-start.4) | async-done | bytes 2228256 | tf_op jit(solution)/shard_map/all_to_all | solution.py:376
  342.7 4.8 %all-to-all-start.3 = ((bf16[128,4,2176]{2,1,0:T(4,128)(2,1)}), bf16[128,4,2176]{2,1,0:T(4,128)(2,1)}, u32[]{:S(2)}, u32[]{:S(2)}) async-start(bf16[128,4,2176]{2,1,0:T(4,128)(2,1)} %bitcast.61), calls=%async_computation.3 | async-start | bytes 4456448 | tf_op jit(solution)/shard_map/all_to_all | solution.py:376
  347.7 2.5 shard_map.156
  350.1 29.1 %all-to-all-done.3 = bf16[128,4,2176]{2,1,0:T(4,128)(2,1)} async-done(((bf16[128,4,2176]{2,1,0:T(4,128)(2,1)}), bf16[128,4,2176]{2,1,0:T(4,128)(2,1)}, u32[]{:S(2)}, u32[]{:S(2)}) %all-to-all-start.3) | async-done | bytes 2228256 | tf_op jit(solution)/shard_map/all_to_all | solution.py:376
  379.2 4.0 all-to-all-start.2
  383.2 0.6 fusion.31
  383.8 1.3 fusion.32
  385.8 0.6 compare_reduce_fusion
  386.4 1.3 constant_dynamic-slice_fusion.2
  387.7 4.0 reshape.167
  391.7 4.0 reshape.164
  395.7 15.4 %all-to-all-done.2 = bf16[32,4,64,128]{3,2,1,0:T(8,128)(2,1)S(1)} async-done(((bf16[32,4,64,128]{3,2,1,0:T(8,128)(2,1)}), bf16[32,4,64,128]{3,2,1,0:T(8,128)(2,1)S(1)}, u32[]{:S(2)}, u32[]{:S(2)}) %all-to-all-start.2) | async-done | bytes 2097184 | tf_op jit(solution)/shard_map/all_to_all | solution.py:314
  411.1 0.5 convert_element_type.93
  411.6 0.9 slice_multiply_fusion
  412.6 0.7 copy-done.1
  413.3 0.7 copy-done.2
  413.9 3.0 fusion.7
  416.9 3.0 fusion.9
  (37 shorter events, 1.1 us)
Async XLA Ops:
  0.6 2.2 copy-start.5
  5.0 8.8 %copy-start.3 = (f32[1,2048,128]{2,1,0:T(8,128)S(1)}, f32[1,2048,128]{2,1,0:T(8,128)}, u32[]{:S(2)}) copy-start(f32[1,2048,128]{2,1,0:T(8,128)} %param.17) | copy-start | bytes 3145732
  5.0 25.9 %all-to-all-start = ((bf16[32,2,64,128]{3,2,1,0:T(8,128)(2,1)}), bf16[32,2,64,128]{3,2,1,0:T(8,128)(2,1)S(1)}, u32[]{:S(2)}, u32[]{:S(2)}) async-start(bf16[32,2,64,128]{3,2,1,0:T(8,128)(2,1)} %pad_maximum_fusion.3), calls=%async_computation | async-start | bytes 2097152 | tf_op jit(solution)/shard_map/all_to_all | solution.py:314
  13.8 2.7 copy-start.4
  18.2 16.7 %copy-start.7 = (s32[16]{0:T(128)S(1)}, s32[16]{0:T(128)}, u32[]{:S(2)}) copy-start(s32[16]{0:T(128)} %param.20) | copy-start | bytes 196
  30.9 273.2 %all-to-all-start.1 = ((bf16[32,4,64,128]{3,2,1,0:T(8,128)(2,1)}), bf16[32,4,64,128]{3,2,1,0:T(8,128)(2,1)S(1)}, u32[]{:S(2)}, u32[]{:S(2)}) async-start(bf16[32,4,64,128]{3,2,1,0:T(8,128)(2,1)} %pad_maximum_fusion.2), calls=%async_computation.1 | async-start | bytes 4194304 | tf_op jit(solution)/shard_map/all_to_all | solution.py:314
  36.9 177.3 %copy-start = (s32[24]{0:T(128)S(1)}, s32[24]{0:T(128)}, u32[]{:S(2)}) copy-start(s32[24]{0:T(128)} %map_ref.3) | copy-start | bytes 292
  255.7 41.3 %copy-start.6 = (s32[24]{0:T(128)S(1)}, s32[24]{0:T(128)}, u32[]{:S(2)}) copy-start(s32[24]{0:T(128)} %param.21) | copy-start | bytes 292
  304.1 38.6 %all-to-all-start.4 = ((bf16[128,4,2176]{2,1,0:T(4,128)(2,1)}), bf16[128,4,2176]{2,1,0:T(4,128)(2,1)}, u32[]{:S(2)}, u32[]{:S(2)}) async-start(bf16[128,4,2176]{2,1,0:T(4,128)(2,1)} %bitcast.60), calls=%async_computation.4 | async-start | bytes 4456448 | tf_op jit(solution)/shard_map/all_to_all | solution.py:376
  342.7 36.6 %all-to-all-start.3 = ((bf16[128,4,2176]{2,1,0:T(4,128)(2,1)}), bf16[128,4,2176]{2,1,0:T(4,128)(2,1)}, u32[]{:S(2)}, u32[]{:S(2)}) async-start(bf16[128,4,2176]{2,1,0:T(4,128)(2,1)} %bitcast.61), calls=%async_computation.3 | async-start | bytes 4456448 | tf_op jit(solution)/shard_map/all_to_all | solution.py:376
  379.2 31.9 %all-to-all-start.2 = ((bf16[32,4,64,128]{3,2,1,0:T(8,128)(2,1)}), bf16[32,4,64,128]{3,2,1,0:T(8,128)(2,1)S(1)}, u32[]{:S(2)}, u32[]{:S(2)}) async-start(bf16[32,4,64,128]{3,2,1,0:T(8,128)(2,1)} %bitcast.15), calls=%async_computation.2 | async-start | bytes 4194304 | tf_op jit(solution)/shard_map/all_to_all | solution.py:314
  411.6 1.6 copy-start.1
  411.6 2.3 copy-start.2

commit v3 on v2

v3 whole, which is shorter than its diff:
```python
import jax
import jax.numpy as jnp
from jax import lax
from jax.experimental import pallas as pl
from jax.experimental.pallas import tpu as pltpu
from jax.sharding import Mesh
from jax.sharding import PartitionSpec as P

epsilon = 1e-05
beta_one = 0.9
beta_two = 0.95
step_rate = 0.003
adam_floor = 1e-08
f32 = jnp.float32
bf16 = jnp.bfloat16
section = ("y", "x", "c")
both = ("y", "x", "c", "z")
orders = (("x", "y", "z"), ("y", "z", "x"), ("z", "x", "y"))
ring = 4
groups = 3
rows = 8
MESH = pl.DeviceIdType.MESH


def deep_of(units):
    return -(-units // groups)


def forward_layer(x, value, output):
    factor = lax.rsqrt(jnp.mean(x * x, axis=-1, keepdims=True) + epsilon)
    hidden = (x * factor).astype(bf16)
    pre = jnp.dot(hidden, value, preferred_element_type=f32)
    units = jax.nn.silu(pre).astype(bf16)
    mixing = lax.dot_general(units, output, (((1,), (1,)), ((), ())), preferred_element_type=f32)
    return (x + mixing).astype(bf16).astype(f32), hidden, pre, units


def gather_kernel(
    old,
    twice_ref,
    own_ref,
    x_ref,
    out_ref,
    in_ref,
    hid_ref,
    pre_ref,
    unit_ref,
    held,
    state,
    send_one,
    recv_one,
    send,
    recv,
    load_sem,
    own_sem,
):
    deep = deep_of(2 * old)
    me = {a: lax.axis_index(a) for a in both}

    def beside(axis, step):
        size = 2 if axis == "c" else ring
        return {axis: lax.rem(me[axis] + step + size, size)}

    barrier = pltpu.get_barrier_semaphore()
    partners = [beside(a, s) for a in ("x", "y", "z") for s in (1, -1)] + [beside("c", 1)]
    for p in partners:
        pl.semaphore_signal(barrier, inc=1, device_id=p, device_id_type=MESH)
    pl.semaphore_wait(barrier, len(partners))

    def copy(src, dst, to, send_sem, recv_sem):
        return pltpu.make_async_remote_copy(
            src_ref=src,
            dst_ref=dst,
            send_sem=send_sem,
            recv_sem=recv_sem,
            device_id=to,
            device_id_type=MESH,
        )

    def place(g, phase, k, at, half):
        full = orders[g][:phase]
        axis = orders[g][phase]
        index = dict(me)
        for a in full:
            index[a] = pl.ds(0, ring)
        if half is not None and full:
            index[full[0]] = pl.ds(half * (ring // 2), ring // 2)
        index[axis] = at
        return out_ref.at[g, k, me["c"], index["x"], index["y"], index["z"]]

    def bulk_first(g):
        axis = orders[g][0]
        dst = place(g, 0, pl.ds(0, deep), me[axis], None)
        return [
            copy(own_ref.at[g], dst, beside(axis, s), send_one.at[g, n], recv_one.at[g, n])
            for n, s in ((0, 1), (1, -1))
        ]

    def bulk_second(g):
        axis = orders[g][0]
        cut = deep // 2
        out = []
        for n, s, lo, size in ((2, 1, 0, cut), (3, -1, cut, deep - cut)):
            part = place(g, 0, pl.ds(lo, size), lax.rem(me[axis] - s + ring, ring), None)
            out.append(copy(part, part, beside(axis, s), send_one.at[g, n], recv_one.at[g, n]))
        return out

    def first(g, phase, k):
        axis = orders[g][phase]
        here = place(g, phase, k, me[axis], None)
        base = 4 * (phase - 1)
        return [
            copy(here, here, beside(axis, s), send.at[g, k, base + n], recv.at[g, k, base + n])
            for n, s in ((0, 1), (1, -1))
        ]

    def second(g, phase, k):
        axis = orders[g][phase]
        base = 4 * (phase - 1) + 2
        out = []
        for n, s in ((0, 1), (1, -1)):
            part = place(g, phase, k, lax.rem(me[axis] - s + ring, ring), n)
            out.append(copy(part, part, beside(axis, s), send.at[g, k, base + n], recv.at[g, k, base + n]))
        return out

    def cross(g, k):
        block = out_ref.at[g, k, me["c"]]
        return [copy(block, block, beside("c", 1), send.at[g, k, 8], recv.at[g, k, 8])]

    def start(copies):
        for c in copies:
            c.start()

    def arrived(copies):
        for c in copies:
            c.wait_recv()

    def each(k, before, after, *more):
        for g in range(groups):
            if before is not None:
                arrived(before(g, *more, k))
            start(after(g, *more, k))

    def spread_start(k):
        each(k, None, lambda g, k: first(g, 1, k))

    def spread_pass(k):
        each(k, lambda g, k: first(g, 1, k), lambda g, k: second(g, 1, k))

    def plane_start(k):
        each(k, lambda g, k: second(g, 1, k), lambda g, k: first(g, 2, k))

    def plane_pass(k):
        each(k, lambda g, k: first(g, 2, k), lambda g, k: second(g, 2, k))

    def cross_start(k):
        each(k, lambda g, k: second(g, 2, k), cross)

    def load(g, k):
        unit = groups * k + g
        layer = lax.div(unit, 2)
        return pltpu.make_async_copy(
            out_ref.at[g, k], held.at[lax.rem(layer, 2), lax.rem(unit, 2)], load_sem.at[g]
        )

    def evaluate(q, carry):
        layer = lax.div(q, 2)
        again = lax.rem(q, 2)
        slot = lax.rem(layer, 2)
        x = state[...]
        following, hidden, pre, units = forward_layer(x, wide(held[slot, 0]), wide(held[slot, 1]))
        in_ref[q] = x.astype(bf16)
        hid_ref[q] = hidden
        pre_ref[q] = pre
        unit_ref[q] = units
        keep = jnp.maximum(twice_ref[layer], 1 - again) > 0
        state[...] = jnp.where(keep, following, x)
        return carry

    def use(k):
        for g in range(groups):
            arrived(cross(g, k))
            load(g, k).start()
        for g in range(groups):
            load(g, k).wait()
        done = jnp.minimum(lax.div(groups * k + groups, 2), old)
        lax.fori_loop(2 * lax.div(groups * k, 2), 2 * done, evaluate, 0)

    mine = pltpu.make_async_copy(
        own_ref, out_ref.at[:, :, me["c"], me["x"], me["y"], me["z"]], own_sem
    )
    mine.start()
    for g in range(groups):
        start(bulk_first(g))
    state[...] = x_ref[...]
    for g in range(groups):
        arrived(bulk_first(g))
        start(bulk_second(g))
    mine.wait()
    for g in range(groups):
        arrived(bulk_second(g))
    for k in range(4):
        spread_start(k)
    for k in range(3):
        spread_pass(k)
    for k in range(2):
        plane_start(k)

    def step(t, carry):
        def at(k, act):
            @pl.when((k >= 0) & (k < deep))
            def _():
                act(k)

        at(t, plane_pass)
        at(t + 2, plane_start)
        at(t + 3, spread_pass)
        at(t + 4, spread_start)
        at(t - 1, cross_start)
        at(t - 2, use)
        return carry

    lax.fori_loop(0, deep + 2, step, 0)

    for g in range(groups):
        for c in bulk_first(g) + bulk_second(g):
            c.wait_send()

    def drain(k, carry):
        for g in range(groups):
            for phase in (1, 2):
                for c in first(g, phase, k) + second(g, phase, k):
                    c.wait_send()
            for c in cross(g, k):
                c.wait_send()
        return carry

    lax.fori_loop(0, deep, drain, 0)


def gather_forward(twice, own, x):
    old = twice.shape[0]
    deep, part, channels = own.shape[-3:]
    features = x.shape[1]
    inner = ring * channels
    shape = jax.ShapeDtypeStruct
    vmem = pl.BlockSpec(memory_space=pltpu.VMEM)
    hbm = pl.BlockSpec(memory_space=pl.ANY)
    unit = (2, ring, ring, ring, part, channels)
    return pl.pallas_call(
        lambda *refs: gather_kernel(old, *refs),
        in_specs=[pl.BlockSpec(memory_space=pltpu.SMEM), hbm, vmem],
        out_specs=[hbm, vmem, vmem, vmem, vmem],
        out_shape=[
            shape(own.shape[:2] + unit, bf16),
            shape((2 * old, rows, features), bf16),
            shape((2 * old, rows, features), bf16),
            shape((2 * old, rows, inner), f32),
            shape((2 * old, rows, inner), bf16),
        ],
        scratch_shapes=[
            pltpu.VMEM((2, 2) + unit, bf16),
            pltpu.VMEM(x.shape, f32),
            pltpu.SemaphoreType.DMA((groups, 4)),
            pltpu.SemaphoreType.DMA((groups, 4)),
            pltpu.SemaphoreType.DMA((groups, deep, 9)),
            pltpu.SemaphoreType.DMA((groups, deep, 9)),
            pltpu.SemaphoreType.DMA((groups,)),
            pltpu.SemaphoreType.DMA,
        ],
        compiler_params=pltpu.CompilerParams(
            collective_id=0, has_side_effects=True, vmem_limit_bytes=48 * 2**20
        ),
        cost_estimate=pl.CostEstimate(
            flops=2 * old * rows * 8 * features * inner // 2,
            bytes_accessed=400 * 2**20,
            transcendentals=0,
        ),
    )(twice, own, x)


def wide(w):
    w = w.reshape((-1,) + w.shape[-3:])
    return jnp.concatenate([w[:, z].reshape(-1, w.shape[-1]) for z in range(w.shape[1])], axis=1)


def backward_kernel(map_ref, place_ref, g_ref, v_ref, o_ref, in_ref, pre_ref, out_g_ref, out_z_ref, state):
    @pl.when(pl.program_id(0) == 0)
    def _():
        state[...] = g_ref[...]

    g = state[...]
    gb = g.astype(bf16)
    out_g_ref[0] = gb
    gu = jnp.dot(gb, wide(o_ref[...]), preferred_element_type=f32)
    pre = pre_ref[0]
    s = jax.nn.sigmoid(pre)
    gz = (gu * s * (1.0 + pre * (1.0 - s))).astype(bf16)
    out_z_ref[0] = gz
    gh = lax.dot_general(gz, wide(v_ref[...]), (((1,), (1,)), ((), ())), preferred_element_type=f32)
    x = in_ref[0].astype(f32)
    factor = lax.rsqrt(jnp.mean(x * x, axis=-1, keepdims=True) + epsilon)
    n = x * factor
    gs = factor * (gh - n * jnp.mean(gh * n, axis=-1, keepdims=True))
    state[...] = (g + gs).astype(bf16).astype(f32)


def run_backward(layer_map, place_of, start, weights, extra):
    new = layer_map.shape[0]
    wshape = weights.shape

    def per_layer(a):
        return pl.BlockSpec((1,) + a.shape[1:], lambda j, m, p: (p[new - 1 - j], 0, 0))

    def half(which):
        def index(j, m, p):
            unit = 2 * m[new - 1 - j] + which
            return (lax.rem(unit, groups), lax.div(unit, groups), 0, 0, 0, 0)

        return pl.BlockSpec((1, 1) + wshape[2:], index)

    size = 4 * wshape[2] * wshape[3] * wshape[4] * wshape[5]
    outs = [jax.ShapeDtypeStruct((new,) + a.shape[1:], bf16) for a in extra]

    def by_layer(a):
        return pl.BlockSpec((1,) + a.shape[1:], lambda j, m, p: (new - 1 - j, 0, 0))
    return pl.pallas_call(
        backward_kernel,
        grid_spec=pltpu.PrefetchScalarGridSpec(
            num_scalar_prefetch=2,
            grid=(new,),
            in_specs=[pl.BlockSpec(start.shape, lambda j, m, p: (0, 0)), half(0), half(1)]
            + [per_layer(a) for a in extra],
            out_specs=[by_layer(a) for a in outs],
            scratch_shapes=[pltpu.VMEM(start.shape, f32)],
        ),
        out_shape=outs,
        compiler_params=pltpu.CompilerParams(
            dimension_semantics=("arbitrary",), vmem_limit_bytes=48 * 2**20
        ),
        cost_estimate=pl.CostEstimate(
            flops=new * 4 * rows * size // 4, bytes_accessed=new * size, transcendentals=0
        ),
    )(layer_map, place_of, start, weights, weights, *extra)


def pick_kernel(index_ref, keep_ref, in_ref, out_ref):
    def one(k, carry):
        kept = in_ref[index_ref[k]] * keep_ref[k].astype(f32).astype(bf16)
        out_ref[k] = kept
        return carry

    lax.fori_loop(0, out_ref.shape[0], one, 0)


def pick_slots(index, keep, pieces):
    whole = pl.BlockSpec(memory_space=pltpu.VMEM)
    scalar = pl.BlockSpec(memory_space=pltpu.SMEM)
    flat = pieces.reshape(pieces.shape[0], -1, pieces.shape[-1])
    got = pl.pallas_call(
        pick_kernel,
        in_specs=[scalar, scalar, whole],
        out_specs=whole,
        out_shape=jax.ShapeDtypeStruct((index.shape[0],) + flat.shape[1:], bf16),
        compiler_params=pltpu.CompilerParams(vmem_limit_bytes=24 * 2**20),
    )(index, keep, flat)
    return got.reshape((index.shape[0],) + pieces.shape[1:])


def pick(onehot, pieces):
    flat = pieces.reshape(pieces.shape[0], -1, pieces.shape[-1])
    got = lax.dot_general(onehot, flat, (((1,), (0,)), ((), ())), preferred_element_type=bf16)
    return got.reshape((onehot.shape[0],) + pieces.shape[1:])


def adam_update(weight, first, second, gradient, owned):
    first_new = beta_one * first + (1.0 - beta_one) * gradient
    second_new = beta_two * second + (1.0 - beta_two) * gradient * gradient
    weight_new = weight - step_rate * first_new / (jnp.sqrt(second_new) + adam_floor)
    weight_new = jnp.where(owned, weight_new, 0.0).astype(bf16)
    return (weight_new[None], first_new[None], second_new[None])


def body(
    tokens,
    cotangent,
    value_weight,
    output_weight,
    value_first,
    output_first,
    value_second,
    output_second,
    layer_map,
    old_section,
    new_section,
):
    sections = lax.axis_size(section)
    width = lax.axis_size("z")
    myself = lax.axis_index(section)
    column = lax.axis_index("z")
    new = new_section.shape[0]
    features, channels = value_weight.shape[1:]
    part = features // sections
    positions = lax.iota(jnp.int32, sections)
    owner_match = positions[:, None] == new_section[None, :]
    map_match = layer_map[:, None] == lax.iota(jnp.int32, old_section.shape[0])[None, :]
    source = jnp.sum(jnp.where(map_match, old_section[None, :], 0), axis=1)
    holds = jnp.any(owner_match, axis=1)
    wanted = jnp.sum(jnp.where(owner_match, source[None, :], 0), axis=1)
    owned = jnp.any(new_section == myself)
    my_layer = jnp.sum(jnp.where(new_section == myself, lax.iota(jnp.int32, new), 0))
    my_old = jnp.sum(jnp.where(lax.iota(jnp.int32, new) == my_layer, layer_map, 0))

    def pieces_of(arrays):
        return jnp.stack([a.reshape(sections, part, channels).astype(bf16) for a in arrays], axis=1)

    def spread(a):
        return lax.all_to_all(a, section, split_axis=0, concat_axis=0, tiled=True)

    def turned(a):
        return a.reshape(2, ring, ring, part * channels).transpose(2, 1, 0, 3)

    old = old_section.shape[0]
    pieces = spread(pieces_of((turned(value_weight), turned(output_weight))))
    deep = deep_of(2 * old)
    unit = jnp.minimum(
        groups * lax.iota(jnp.int32, deep)[None, :] + lax.iota(jnp.int32, groups)[:, None], 2 * old - 1
    ).reshape(-1)
    unit_match = (unit // 2)[:, None] == lax.iota(jnp.int32, old)[None, :]
    slots = 2 * jnp.sum(jnp.where(unit_match, old_section[None, :], 0), axis=1) + unit % 2
    own = pick_slots(slots, jnp.ones_like(slots), pieces.reshape(2 * sections, part, channels))
    count = tokens.shape[0] // sections

    def mine(a):
        block = lax.dynamic_slice_in_dim(a, myself * count, count, axis=0).astype(f32)
        return jnp.pad(block, ((0, rows - count), (0, 0)))

    numbers = lax.iota(jnp.int32, old)
    twice = (jnp.sum((layer_map[:, None] == numbers[None, :]).astype(jnp.int32), axis=0) > 1).astype(jnp.int32)
    before = jnp.concatenate([jnp.full((1,), -1, jnp.int32), layer_map[:-1]])
    place_of = 2 * layer_map + (before == layer_map).astype(jnp.int32)
    gathered, saved_in, hidden, pre, units = gather_forward(
        twice, own.reshape(groups, deep, part, channels), mine(tokens)
    )
    gathered = gathered.reshape(groups, deep, sections, width, part, channels)
    moments = pick_slots(
        wanted,
        holds.astype(jnp.int32),
        spread(pieces_of((value_first, output_first, value_second, output_second))),
    )

    send_place = jnp.sum(jnp.where(owner_match, place_of[None, :], 0), axis=1)
    places = lax.iota(jnp.int32, 2 * old)
    send_layer = ((send_place[:, None] == places[None, :]) & holds[:, None]).astype(bf16)

    def message(choice, wide, narrow):
        w = pick(choice, wide[:, :count])
        n = pick(choice, narrow[:, :count])
        n = n.reshape(sections, count, width, channels).transpose(0, 2, 1, 3)
        w = jnp.broadcast_to(w[:, None], (sections, width, count, features))
        return jnp.concatenate([w, n], axis=-1).reshape(sections * width, count, features + channels)

    def to_owner(sent):
        got = lax.all_to_all(sent, both, split_axis=0, concat_axis=0, tiled=True)
        got = got.reshape(sections * width * count, features + channels)
        return got[:, :features], got[:, features:]

    forward_sent = message(send_layer, hidden, units)
    entering = mine(cotangent)
    forward_sent, moments, entering = lax.optimization_barrier((forward_sent, moments, entering))
    hidden_all, units_all = to_owner(forward_sent)
    grads, inner_grads = run_backward(layer_map, place_of, entering, gathered, (saved_in, pre))
    grads_all, inner_all = to_owner(message(owner_match.astype(bf16), grads, inner_grads))
    moments, hidden_all = lax.optimization_barrier((moments, hidden_all))
    moments = spread(moments)

    def weight_grad(a, b):
        return lax.dot_general(a, b, (((0,), (0,)), ((), ())), preferred_element_type=f32)

    grad_value = weight_grad(hidden_all, inner_all)
    grad_output = weight_grad(grads_all, units_all)
    def own_of(which):
        unit = 2 * my_old + which
        got = lax.dynamic_slice(
            gathered,
            (unit % groups, unit // groups, 0, column, 0, 0),
            (1, 1, sections, 1, part, channels),
        )
        return got.reshape(features, channels).astype(f32)

    moments = moments.astype(f32)

    def full(a):
        return a.reshape(features, channels)

    value_new = adam_update(own_of(0), full(moments[:, 0]), full(moments[:, 2]), grad_value, owned)
    output_new = adam_update(own_of(1), full(moments[:, 1]), full(moments[:, 3]), grad_output, owned)
    return (value_new[0], output_new[0], value_new[1], output_new[1], value_new[2], output_new[2])


def solution(mesh):
    split = P(section, None, "z")
    placed = (P("z", None),) * 2 + (split,) * 6 + (P(),) * 3
    fine = Mesh(mesh.devices.reshape(ring, ring, 2, ring), both)
    return jax.shard_map(body, mesh=fine, in_specs=placed, out_specs=(split,) * 6, check_vma=False)
```

time: 422 us -> 368 us (0.87)
  Pallas kernels: 263 us -> 221 us
  waiting for transfers between devices: 83.4 us -> 62.2 us
  starting transfers between devices: 28.4 us -> 34.6 us
    pallas_call x3 -> x2, Pallas kernels: 260 us -> 218 us  [the longest x1 176 us: gather_forward(): pl.pallas_call(lambda *refs: gather_kernel(old, *refs), in_specs=[pl.Bloc...]
    all_to_all x2, waiting for transfers between devices: 55.3 us -> 27.9 us  [to_owner(): got = lax.all_to_all(sent, both, split_axis=0, concat_axis=0, tiled=True)]
    all_to_all x3, waiting for transfers between devices: 28.1 us -> 34.3 us  [spread(): return lax.all_to_all(a, section, split_axis=0, concat_axis=0, tiled=True)]
    all_to_all x2, starting transfers between devices: 11.7 us -> 17.3 us  [to_owner(): got = lax.all_to_all(sent, both, split_axis=0, concat_axis=0, tiled=True)]
    unnamed x16 -> x34, local copies, waits for them, and re-layouts: 1.41 us -> 6.83 us
  transfers between devices with their start and end apart: 5 -> 5, of which waited for: 4 -> 3; matrix products, arithmetic and copies ran while one was open for 7% -> 7% of each run, Pallas kernels for 63% -> 60%
where the time goes in v3:
time: 368 us; the launch traced here: 366 us
  Pallas kernels  221 us (60%)
  waiting for transfers between devices  62.2 us (17%)
  starting transfers between devices  34.6 us (9%)
  local copies, waits for them, and re-layouts  24 us (7%)
  other arithmetic  13.9 us (4%)
  matrix products  8.34 us (2%)
    pallas_call x1, Pallas kernels, gather_forward(): pl.pallas_call(lambda *refs: gather_kernel(old, *refs), in_specs=[pl.Bloc...  176 us
    pallas_call x1, Pallas kernels, run_backward(): pl.pallas_call(backward_kernel, grid_spec=pltpu.PrefetchScalarGridSpec(nu...  41.7 us
    all_to_all x3, waiting for transfers between devices, spread(): return lax.all_to_all(a, section, split_axis=0, concat_axis=0, tiled=True)  34.3 us
    all_to_all x2, waiting for transfers between devices, to_owner(): got = lax.all_to_all(sent, both, split_axis=0, concat_axis=0, tiled=True)  27.9 us
    all_to_all x2, starting transfers between devices, to_owner(): got = lax.all_to_all(sent, both, split_axis=0, concat_axis=0, tiled=True)  17.3 us
    all_to_all x3, starting transfers between devices, spread(): return lax.all_to_all(a, section, split_axis=0, concat_axis=0, tiled=True)  17.3 us
  transfers between devices with their start and end apart: 5, of which 3 were waited for; matrix products, arithmetic and copies ran while one was open for 7% of the time, Pallas kernels for 60%

profile of v3, /device:TPU:1, one launch (start us, length us, event | category | flops | bytes accessed | tf_op | source)
XLA Modules:
  0.0 366.4 jit_solution(10844965593841670312)
XLA Ops:
  0.7 1.3 reshape.158
  1.9 0.5 copy.31
  2.5 0.4 stack_reshape.6
  3.0 0.5 copy.32
  3.6 0.4 stack_reshape.7
  4.0 1.1 pad_maximum_fusion.3
  5.1 8.6 %all-to-all-start = ((bf16[32,2,64,128]{3,2,1,0:T(8,128)(2,1)}), bf16[32,2,64,128]{3,2,1,0:T(8,128)(2,1)S(1)}, u32[]{:S(2)}, u32[]{:S(2)}) async-start(bf16[32,2,64,128]{3,2,1,0:T(8,128)(2,1)} %pad_maximum_fusion.3), calls=%async_computation | async-start | bytes 2097152 | tf_op jit(solution)/shard_map/all_to_all | solution.py:418
  14.0 0.6 fusion.34
  14.7 0.4 copy-done.10
  15.4 0.6 copy-done.12
  16.1 1.6 pad_maximum_fusion.2
  17.7 1.3 fusion.36
  19.0 11.8 %all-to-all-done = bf16[32,2,64,128]{3,2,1,0:T(8,128)(2,1)S(1)} async-done(((bf16[32,2,64,128]{3,2,1,0:T(8,128)(2,1)}), bf16[32,2,64,128]{3,2,1,0:T(8,128)(2,1)S(1)}, u32[]{:S(2)}, u32[]{:S(2)}) %all-to-all-start) | async-done | bytes 1048608 | tf_op jit(solution)/shard_map/all_to_all | solution.py:418
  30.9 1.0 copy-done.1
  31.8 4.1 %all-to-all-start.1 = ((bf16[32,4,64,128]{3,2,1,0:T(8,128)(2,1)}), bf16[32,4,64,128]{3,2,1,0:T(8,128)(2,1)S(1)}, u32[]{:S(2)}, u32[]{:S(2)}) async-start(bf16[32,4,64,128]{3,2,1,0:T(8,128)(2,1)} %pad_maximum_fusion.2), calls=%async_computation.1 | async-start | bytes 4194304 | tf_op jit(solution)/shard_map/all_to_all | solution.py:418
  36.1 0.8 constant_dynamic-slice_fusion
  36.9 1.2 copy-done.2
  38.2 1.0 shard_map.154
  39.2 176.4 %shard_map.155 = (bf16[3,11,2,4,4,4,64,128]{7,6,5,4,3,2,1,0:T(8,128)(2,1)}, bf16[32,8,2048]{2,1,0:T(8,128)(2,1)S(1)}, bf16[32,8,2048]{2,1,0:T(8,128)(2,1)S(1)}, ...) custom-call(s32[16]{0:T(128)S(1)} %compare_convert_fusion.1.refs_0_, bf16[3,11,64,128]{3,2,1,0:T(8,128)(2,1)S(1)} %bitcast.63, ...), custom_call_target="tpu_custom_call" | custom-call | flops 1073741824 | bytes 419430400 | tf_op jit(solution)/shard_map/pallas_call | solution.py:250
  215.5 1.0 copy-done.3
  216.5 1.0 copy-done.5
  217.9 1.5 slice.40
  219.3 0.8 fusion.8
  220.1 0.4 copy.34
  220.5 1.0 broadcast_in_dim.105
  221.6 2.6 pad_maximum_fusion
  224.1 2.5 shard_map.156
  226.6 7.6 %all-to-all-start.2 = ((bf16[128,4,2176]{2,1,0:T(4,128)(2,1)}), bf16[128,4,2176]{2,1,0:T(4,128)(2,1)}, u32[]{:S(2)}, u32[]{:S(2)}) async-start(bf16[128,4,2176]{2,1,0:T(4,128)(2,1)} %bitcast.65), calls=%async_computation.2 | async-start | bytes 4456448 | tf_op jit(solution)/shard_map/all_to_all | solution.py:464
  234.2 41.7 %shard_map.157 = (bf16[24,8,2048]{2,1,0:T(8,128)(2,1)S(1)}, bf16[24,8,512]{2,1,0:T(8,128)(2,1)S(1)}) custom-call(s32[24]{0:T(128)S(1)} %copy-done.6, s32[24]{0:T(128)S(1)} %get-tuple-element.46.place_ref, f32[8,2048]{1,0:T(8,128)S(1)} %pad_convert_fusion.g_ref, bf16[3,11,32,4,64,128]{5,4,3,2,1,0:T(8,128)(2,1)} %bitcast.4.v_ref.o_ref, ...), custom_call_target="tpu_custom_call" | custom-call | flops 805306368 | bytes 100663296 | tf_op jit(solution)/shard_map/pallas_call | solution.py:327
  276.1 0.3 fusion.17
  276.5 0.7 fusion.10
  277.2 0.4 copy.42
  277.6 1.0 broadcast_in_dim.109
  278.7 2.5 pad_maximum_fusion.1
  281.2 9.8 %all-to-all-start.4 = ((bf16[128,4,2176]{2,1,0:T(4,128)(2,1)}), bf16[128,4,2176]{2,1,0:T(4,128)(2,1)S(1)}, u32[]{:S(2)}, u32[]{:S(2)}) async-start(bf16[128,4,2176]{2,1,0:T(4,128)(2,1)} %bitcast.66), calls=%async_computation.4 | async-start | bytes 4456448 | tf_op jit(solution)/shard_map/all_to_all | solution.py:464
  291.0 4.0 %reshape.167 = bf16[512,2176]{1,0:T(8,128)(2,1)} reshape(bf16[128,4,2176]{2,1,0:T(4,128)(2,1)} %all-to-all-done.2) | data formatting | bytes 4456448 | tf_op jit(solution)/shard_map/reshape | solution.py:465
  295.0 27.9 %all-to-all-done.4 = bf16[128,4,2176]{2,1,0:T(4,128)(2,1)S(1)} async-done(((bf16[128,4,2176]{2,1,0:T(4,128)(2,1)}), bf16[128,4,2176]{2,1,0:T(4,128)(2,1)S(1)}, u32[]{:S(2)}, u32[]{:S(2)}) %all-to-all-start.4) | async-done | bytes 2228256 | tf_op jit(solution)/shard_map/all_to_all | solution.py:464
  322.9 4.7 %all-to-all-start.3 = ((bf16[32,4,64,128]{3,2,1,0:T(8,128)(2,1)}), bf16[32,4,64,128]{3,2,1,0:T(8,128)(2,1)}, u32[]{:S(2)}, u32[]{:S(2)}) async-start(bf16[32,4,64,128]{3,2,1,0:T(8,128)(2,1)} %bitcast.18), calls=%async_computation.3 | async-start | bytes 4194304 | tf_op jit(solution)/shard_map/all_to_all | solution.py:418
  328.3 0.6 compare_reduce_fusion
  329.0 2.1 constant_dynamic-slice_fusion.3
  331.0 2.1 reshape.170
  333.1 22.5 %all-to-all-done.3 = bf16[32,4,64,128]{3,2,1,0:T(8,128)(2,1)} async-done(((bf16[32,4,64,128]{3,2,1,0:T(8,128)(2,1)}), bf16[32,4,64,128]{3,2,1,0:T(8,128)(2,1)}, u32[]{:S(2)}, u32[]{:S(2)}) %all-to-all-start.3) | async-done | bytes 2097184 | tf_op jit(solution)/shard_map/all_to_all | solution.py:418
  355.6 2.1 convert_element_type.106
  357.7 0.9 slice_multiply_fusion
  358.6 0.7 copy-done.7
  359.3 0.7 copy-done.8
  360.0 3.2 fusion.5
  363.2 3.1 fusion.7
  (58 shorter events, 2.1 us)
Async XLA Ops:
  0.6 35.4 %copy-start = (bf16[128,2048]{1,0:T(8,128)(2,1)S(1)}, bf16[128,2048]{1,0:T(8,128)(2,1)}, u32[]{:S(2)}) copy-start(bf16[128,2048]{1,0:T(8,128)(2,1)} %param.11) | copy-start | bytes 1572868
  0.6 2.2 copy-start.13
  4.0 9.8 %copy-start.6 = (s32[24]{0:T(128)S(1)}, s32[24]{0:T(128)}, u32[]{:S(2)}) copy-start(s32[24]{0:T(128)} %map_ref.1) | copy-start | bytes 292
  4.0 9.8 %copy-start.16 = (s32[16]{0:T(128)S(1)}, s32[16]{0:T(128)}, u32[]{:S(2)}) copy-start(s32[16]{0:T(128)} %param.20) | copy-start | bytes 196
  4.0 10.0 %copy-start.15 = (s32[24]{0:T(128)S(1)}, s32[24]{0:T(128)}, u32[]{:S(2)}) copy-start(s32[24]{0:T(128)} %param.21) | copy-start | bytes 292
  4.0 10.6 %copy-start.9 = (f32[1,2048,128]{2,1,0:T(8,128)S(1)}, f32[1,2048,128]{2,1,0:T(8,128)}, u32[]{:S(2)}) copy-start(f32[1,2048,128]{2,1,0:T(8,128)} %param.15) | copy-start | bytes 3145732
  5.1 25.8 %all-to-all-start = ((bf16[32,2,64,128]{3,2,1,0:T(8,128)(2,1)}), bf16[32,2,64,128]{3,2,1,0:T(8,128)(2,1)S(1)}, u32[]{:S(2)}, u32[]{:S(2)}) async-start(bf16[32,2,64,128]{3,2,1,0:T(8,128)(2,1)} %pad_maximum_fusion.3), calls=%async_computation | async-start | bytes 2097152 | tf_op jit(solution)/shard_map/all_to_all | solution.py:418
  13.8 1.2 copy-start.10
  13.8 1.5 copy-start.11
  14.6 1.4 copy-start.12
  30.8 1.0 copy-start.1
  31.8 192.3 %all-to-all-start.1 = ((bf16[32,4,64,128]{3,2,1,0:T(8,128)(2,1)}), bf16[32,4,64,128]{3,2,1,0:T(8,128)(2,1)S(1)}, u32[]{:S(2)}, u32[]{:S(2)}) async-start(bf16[32,4,64,128]{3,2,1,0:T(8,128)(2,1)} %pad_maximum_fusion.2), calls=%async_computation.1 | async-start | bytes 4194304 | tf_op jit(solution)/shard_map/all_to_all | solution.py:418
  36.9 1.2 copy-start.2
  215.5 1.0 copy-start.3
  216.5 1.0 copy-start.5
  226.6 7.6 %copy-start.4 = (bf16[32,8,2048]{2,1,0:T(8,128)(2,1)S(1)}, bf16[32,8,2048]{2,1,0:T(8,128)(2,1)}, u32[]{:S(2)}) copy-start(bf16[32,8,2048]{2,1,0:T(8,128)(2,1)} %copy-done.3) | copy-start | bytes 3145732
  226.6 54.6 %all-to-all-start.2 = ((bf16[128,4,2176]{2,1,0:T(4,128)(2,1)}), bf16[128,4,2176]{2,1,0:T(4,128)(2,1)}, u32[]{:S(2)}, u32[]{:S(2)}) async-start(bf16[128,4,2176]{2,1,0:T(4,128)(2,1)} %bitcast.65), calls=%async_computation.2 | async-start | bytes 4456448 | tf_op jit(solution)/shard_map/all_to_all | solution.py:464
  281.2 41.7 %all-to-all-start.4 = ((bf16[128,4,2176]{2,1,0:T(4,128)(2,1)}), bf16[128,4,2176]{2,1,0:T(4,128)(2,1)S(1)}, u32[]{:S(2)}, u32[]{:S(2)}) async-start(bf16[128,4,2176]{2,1,0:T(4,128)(2,1)} %bitcast.66), calls=%async_computation.4 | async-start | bytes 4456448 | tf_op jit(solution)/shard_map/all_to_all | solution.py:464
  322.9 32.6 %all-to-all-start.3 = ((bf16[32,4,64,128]{3,2,1,0:T(8,128)(2,1)}), bf16[32,4,64,128]{3,2,1,0:T(8,128)(2,1)}, u32[]{:S(2)}, u32[]{:S(2)}) async-start(bf16[32,4,64,128]{3,2,1,0:T(8,128)(2,1)} %bitcast.18), calls=%async_computation.3 | async-start | bytes 4194304 | tf_op jit(solution)/shard_map/all_to_all | solution.py:418
  357.6 1.6 copy-start.7
  357.7 2.3 copy-start.8
  357.7 2.4 copy-start.14
  360.0 3.2 slice-start

commit v4 on v3

--- a/solution.py
+++ b/solution.py
@@ -19,6 +19,8 @@
 ring = 4
 groups = 3
 rows = 8
+ahead = 4
+early = 3
 MESH = pl.DeviceIdType.MESH
 
 
@@ -88,19 +90,23 @@
         index[axis] = at
         return out_ref.at[g, k, me["c"], index["x"], index["y"], index["z"]]
 
-    def bulk_first(g):
+    spans = ((0, early), (early, deep - early))
+
+    def bulk_first(g, b):
         axis = orders[g][0]
-        dst = place(g, 0, pl.ds(0, deep), me[axis], None)
+        part = pl.ds(*spans[b])
+        dst = place(g, 0, part, me[axis], None)
         return [
-            copy(own_ref.at[g], dst, beside(axis, s), send_one.at[g, n], recv_one.at[g, n])
-            for n, s in ((0, 1), (1, -1))
+            copy(own_ref.at[g, part], dst, beside(axis, s), send_one.at[g, n], recv_one.at[g, n])
+            for n, s in ((4 * b, 1), (4 * b + 1, -1))
         ]
 
-    def bulk_second(g):
+    def bulk_second(g, b):
         axis = orders[g][0]
-        cut = deep // 2
+        lo, size = spans[b]
+        cut = size // 2
         out = []
-        for n, s, lo, size in ((2, 1, 0, cut), (3, -1, cut, deep - cut)):
+        for n, s, lo, size in ((4 * b + 2, 1, lo, cut), (4 * b + 3, -1, lo + cut, size - cut)):
             part = place(g, 0, pl.ds(lo, size), lax.rem(me[axis] - s + ring, ring), None)
             out.append(copy(part, part, beside(axis, s), send_one.at[g, n], recv_one.at[g, n]))
         return out
@@ -190,21 +196,33 @@
         own_ref, out_ref.at[:, :, me["c"], me["x"], me["y"], me["z"]], own_sem
     )
     mine.start()
-    for g in range(groups):
-        start(bulk_first(g))
+    for b in range(2):
+        for g in range(groups):
+            start(bulk_first(g, b))
     state[...] = x_ref[...]
-    for g in range(groups):
-        arrived(bulk_first(g))
-        start(bulk_second(g))
+
+    def bulk_pass(b):
+        for g in range(groups):
+            arrived(bulk_first(g, b))
+            start(bulk_second(g, b))
+
+    def bulk_end(b):
+        for g in range(groups):
+            arrived(bulk_second(g, b))
+
+    bulk_pass(0)
     mine.wait()
-    for g in range(groups):
-        arrived(bulk_second(g))
-    for k in range(4):
+    bulk_end(0)
+    for k in range(early):
         spread_start(k)
-    for k in range(3):
-        spread_pass(k)
-    for k in range(2):
-        plane_start(k)
+    bulk_pass(1)
+    spread_pass(0)
+    spread_pass(1)
+    plane_start(0)
+    bulk_end(1)
+    spread_pass(2)
+    spread_start(3)
+    plane_start(1)
 
     def step(t, carry):
         def at(k, act):
@@ -223,8 +241,9 @@
     lax.fori_loop(0, deep + 2, step, 0)
 
     for g in range(groups):
-        for c in bulk_first(g) + bulk_second(g):
-            c.wait_send()
+        for b in range(2):
+            for c in bulk_first(g, b) + bulk_second(g, b):
+                c.wait_send()
 
     def drain(k, carry):
         for g in range(groups):
@@ -261,8 +280,8 @@
         scratch_shapes=[
             pltpu.VMEM((2, 2) + unit, bf16),
             pltpu.VMEM(x.shape, f32),
-            pltpu.SemaphoreType.DMA((groups, 4)),
-            pltpu.SemaphoreType.DMA((groups, 4)),
+            pltpu.SemaphoreType.DMA((groups, 8)),
+            pltpu.SemaphoreType.DMA((groups, 8)),
             pltpu.SemaphoreType.DMA((groups, deep, 9)),
             pltpu.SemaphoreType.DMA((groups, deep, 9)),
             pltpu.SemaphoreType.DMA((groups,)),
@@ -284,64 +303,93 @@
     return jnp.concatenate([w[:, z].reshape(-1, w.shape[-1]) for z in range(w.shape[1])], axis=1)
 
 
-def backward_kernel(map_ref, place_ref, g_ref, v_ref, o_ref, in_ref, pre_ref, out_g_ref, out_z_ref, state):
-    @pl.when(pl.program_id(0) == 0)
-    def _():
-        state[...] = g_ref[...]
-
-    g = state[...]
+def backward_layer(x, pre, g, value, output):
     gb = g.astype(bf16)
-    out_g_ref[0] = gb
-    gu = jnp.dot(gb, wide(o_ref[...]), preferred_element_type=f32)
-    pre = pre_ref[0]
+    gu = jnp.dot(gb, output, preferred_element_type=f32)
     s = jax.nn.sigmoid(pre)
     gz = (gu * s * (1.0 + pre * (1.0 - s))).astype(bf16)
-    out_z_ref[0] = gz
-    gh = lax.dot_general(gz, wide(v_ref[...]), (((1,), (1,)), ((), ())), preferred_element_type=f32)
-    x = in_ref[0].astype(f32)
+    gh = lax.dot_general(gz, value, (((1,), (1,)), ((), ())), preferred_element_type=f32)
     factor = lax.rsqrt(jnp.mean(x * x, axis=-1, keepdims=True) + epsilon)
     n = x * factor
     gs = factor * (gh - n * jnp.mean(gh * n, axis=-1, keepdims=True))
-    state[...] = (g + gs).astype(bf16).astype(f32)
-
-
-def run_backward(layer_map, place_of, start, weights, extra):
-    new = layer_map.shape[0]
-    wshape = weights.shape
-
-    def per_layer(a):
-        return pl.BlockSpec((1,) + a.shape[1:], lambda j, m, p: (p[new - 1 - j], 0, 0))
-
-    def half(which):
-        def index(j, m, p):
-            unit = 2 * m[new - 1 - j] + which
-            return (lax.rem(unit, groups), lax.div(unit, groups), 0, 0, 0, 0)
-
-        return pl.BlockSpec((1, 1) + wshape[2:], index)
-
-    size = 4 * wshape[2] * wshape[3] * wshape[4] * wshape[5]
-    outs = [jax.ShapeDtypeStruct((new,) + a.shape[1:], bf16) for a in extra]
-
-    def by_layer(a):
-        return pl.BlockSpec((1,) + a.shape[1:], lambda j, m, p: (new - 1 - j, 0, 0))
+    return (g + gs).astype(bf16).astype(f32), gb, gz
+
+
+def backward_kernel(
+    twice_ref, g_ref, weight_ref, in_ref, pre_ref, out_g_ref, out_z_ref, held, state, load_sem
+):
+    old = in_ref.shape[0] // 2
+    new = out_g_ref.shape[0]
+
+    def loads(n):
+        out = []
+        for h in range(2):
+            unit = 2 * (old - 1 - n) + h
+            slot = lax.rem(n, ahead)
+            src = weight_ref.at[lax.rem(unit, groups), lax.div(unit, groups)]
+            out.append(pltpu.make_async_copy(src, held.at[slot, h], load_sem.at[slot, h]))
+        return out
+
+    def start(n):
+        for c in loads(n):
+            c.start()
+
+    for n in range(ahead):
+        start(n)
+    state[...] = g_ref[...]
+
+    def layer(n, j):
+        for c in loads(n):
+            c.wait()
+        slot = lax.rem(n, ahead)
+        i = old - 1 - n
+        extra = twice_ref[i]
+
+        def evaluate(r, j):
+            q = 2 * i + extra - r
+            x = in_ref[q].astype(f32)
+            g, gb, gz = backward_layer(x, pre_ref[q], state[...], wide(held[slot, 0]), wide(held[slot, 1]))
+            out_g_ref[j] = gb
+            out_z_ref[j] = gz
+            state[...] = g
+            return j - 1
+
+        j = lax.fori_loop(0, extra + 1, evaluate, j)
+
+        @pl.when(n + ahead < old)
+        def _():
+            start(n + ahead)
+
+        return j
+
+    lax.fori_loop(0, old, layer, new - 1)
+
+
+def run_backward(new, twice, g, weights, saved_in, pre):
+    shape = jax.ShapeDtypeStruct
+    vmem = pl.BlockSpec(memory_space=pltpu.VMEM)
+    size = 2 * weights.size // (weights.shape[0] * weights.shape[1]) * 2 * twice.shape[0]
     return pl.pallas_call(
         backward_kernel,
-        grid_spec=pltpu.PrefetchScalarGridSpec(
-            num_scalar_prefetch=2,
-            grid=(new,),
-            in_specs=[pl.BlockSpec(start.shape, lambda j, m, p: (0, 0)), half(0), half(1)]
-            + [per_layer(a) for a in extra],
-            out_specs=[by_layer(a) for a in outs],
-            scratch_shapes=[pltpu.VMEM(start.shape, f32)],
+        in_specs=[
+            pl.BlockSpec(memory_space=pltpu.SMEM),
+            vmem,
+            pl.BlockSpec(memory_space=pl.ANY),
+            vmem,
+            vmem,
+        ],
+        out_specs=[vmem, vmem],
+        out_shape=[shape((new,) + a.shape[1:], bf16) for a in (saved_in, pre)],
+        scratch_shapes=[
+            pltpu.VMEM((ahead, 2) + weights.shape[2:], bf16),
+            pltpu.VMEM(g.shape, f32),
+            pltpu.SemaphoreType.DMA((ahead, 2)),
+        ],
+        compiler_params=pltpu.CompilerParams(vmem_limit_bytes=48 * 2**20),
+        cost_estimate=pl.CostEstimate(
+            flops=2 * rows * size, bytes_accessed=2 * size, transcendentals=0
         ),
-        out_shape=outs,
-        compiler_params=pltpu.CompilerParams(
-            dimension_semantics=("arbitrary",), vmem_limit_bytes=48 * 2**20
-        ),
-        cost_estimate=pl.CostEstimate(
-            flops=new * 4 * rows * size // 4, bytes_accessed=new * size, transcendentals=0
-        ),
-    )(layer_map, place_of, start, weights, weights, *extra)
+    )(twice, g, weights, saved_in, pre)
 
 
 def pick_kernel(index_ref, keep_ref, in_ref, out_ref):
@@ -443,11 +491,7 @@
         twice, own.reshape(groups, deep, part, channels), mine(tokens)
     )
     gathered = gathered.reshape(groups, deep, sections, width, part, channels)
-    moments = pick_slots(
-        wanted,
-        holds.astype(jnp.int32),
-        spread(pieces_of((value_first, output_first, value_second, output_second))),
-    )
+    moments = spread(pieces_of((value_first, output_first, value_second, output_second)))
 
     send_place = jnp.sum(jnp.where(owner_match, place_of[None, :], 0), axis=1)
     places = lax.iota(jnp.int32, 2 * old)
@@ -469,9 +513,10 @@
     entering = mine(cotangent)
     forward_sent, moments, entering = lax.optimization_barrier((forward_sent, moments, entering))
     hidden_all, units_all = to_owner(forward_sent)
-    grads, inner_grads = run_backward(layer_map, place_of, entering, gathered, (saved_in, pre))
+    grads, inner_grads = run_backward(new, twice, entering, gathered, saved_in, pre)
     grads_all, inner_all = to_owner(message(owner_match.astype(bf16), grads, inner_grads))
     moments, hidden_all = lax.optimization_barrier((moments, hidden_all))
+    moments = pick_slots(wanted, holds.astype(jnp.int32), moments)
     moments = spread(moments)
 
     def weight_grad(a, b):

time: 368 us -> 351 us (0.954)
  Pallas kernels: 221 us -> 209 us
  waiting for transfers between devices: 62.2 us -> 57.5 us
    pallas_call x1, Pallas kernels: 41.7 us -> 29 us  [run_backward(): pl.pallas_call(backward_kernel, in_specs=[pl.BlockSpec(memory_space=pltpu...]
  transfers between devices with their start and end apart: 5 -> 5, of which waited for: 3 -> 3; matrix products, arithmetic and copies ran while one was open for 7% -> 8% of each run, Pallas kernels for 60% -> 60%
where the time goes in v4:
time: 351 us; the launch traced here: 349 us
  Pallas kernels  209 us (60%)
  waiting for transfers between devices  57.5 us (16%)
  starting transfers between devices  33.1 us (9%)
  local copies, waits for them, and re-layouts  27.2 us (8%)
  other arithmetic  12.3 us (4%)
  matrix products  8.23 us (2%)
    pallas_call x1, Pallas kernels, gather_forward(): pl.pallas_call(lambda *refs: gather_kernel(old, *refs), in_specs=[pl.Bloc...  176 us
    all_to_all x3, waiting for transfers between devices, spread(): return lax.all_to_all(a, section, split_axis=0, concat_axis=0, tiled=True)  32.3 us
    pallas_call x1, Pallas kernels, run_backward(): pl.pallas_call(backward_kernel, in_specs=[pl.BlockSpec(memory_space=pltpu...  29 us
    all_to_all x2, waiting for transfers between devices, to_owner(): got = lax.all_to_all(sent, both, split_axis=0, concat_axis=0, tiled=True)  25.2 us
    all_to_all x3, starting transfers between devices, spread(): return lax.all_to_all(a, section, split_axis=0, concat_axis=0, tiled=True)  16.6 us
    all_to_all x2, starting transfers between devices, to_owner(): got = lax.all_to_all(sent, both, split_axis=0, concat_axis=0, tiled=True)  16.4 us
    reshape x2, local copies, waits for them, and re-layouts, to_owner(): got = got.reshape(sections * width * count, features + channels)  8.06 us
    unnamed x34, local copies, waits for them, and re-layouts  8.06 us
  transfers between devices with their start and end apart: 5, of which 3 were waited for; matrix products, arithmetic and copies ran while one was open for 8% of the time, Pallas kernels for 60%

profile of v4, /device:TPU:1, one launch (start us, length us, event | category | flops | bytes accessed | tf_op | source)
XLA Modules:
  0.0 348.7 jit_solution(12677536269030465020)
XLA Ops:
  0.7 1.3 reshape.158
  1.9 0.5 copy.31
  2.5 0.4 stack_reshape.6
  3.0 0.5 copy.32
  3.6 0.4 stack_reshape.7
  4.0 1.1 pad_maximum_fusion.3
  5.1 8.6 %all-to-all-start = ((bf16[32,2,64,128]{3,2,1,0:T(8,128)(2,1)}), bf16[32,2,64,128]{3,2,1,0:T(8,128)(2,1)S(1)}, u32[]{:S(2)}, u32[]{:S(2)}) async-start(bf16[32,2,64,128]{3,2,1,0:T(8,128)(2,1)} %pad_maximum_fusion.3), calls=%async_computation | async-start | bytes 2097152 | tf_op jit(solution)/shard_map/all_to_all | solution.py:466
  14.0 0.6 fusion.34
  14.7 0.4 copy-done.9
  15.4 0.6 copy-done.11
  16.1 1.6 pad_maximum_fusion.2
  17.7 1.3 fusion.36
  19.0 11.8 %all-to-all-done = bf16[32,2,64,128]{3,2,1,0:T(8,128)(2,1)S(1)} async-done(((bf16[32,2,64,128]{3,2,1,0:T(8,128)(2,1)}), bf16[32,2,64,128]{3,2,1,0:T(8,128)(2,1)S(1)}, u32[]{:S(2)}, u32[]{:S(2)}) %all-to-all-start) | async-done | bytes 1048608 | tf_op jit(solution)/shard_map/all_to_all | solution.py:466
  30.9 1.0 copy-done.1
  31.8 4.1 %all-to-all-start.1 = ((bf16[32,4,64,128]{3,2,1,0:T(8,128)(2,1)}), bf16[32,4,64,128]{3,2,1,0:T(8,128)(2,1)S(1)}, u32[]{:S(2)}, u32[]{:S(2)}) async-start(bf16[32,4,64,128]{3,2,1,0:T(8,128)(2,1)} %pad_maximum_fusion.2), calls=%async_computation.1 | async-start | bytes 4194304 | tf_op jit(solution)/shard_map/all_to_all | solution.py:466
  36.1 0.8 constant_dynamic-slice_fusion
  36.9 1.2 copy-done.2
  38.2 1.0 shard_map.154
  39.1 176.2 %shard_map.155 = (bf16[3,11,2,4,4,4,64,128]{7,6,5,4,3,2,1,0:T(8,128)(2,1)}, bf16[32,8,2048]{2,1,0:T(8,128)(2,1)S(1)}, bf16[32,8,2048]{2,1,0:T(8,128)(2,1)S(1)}, ...) custom-call(s32[16]{0:T(128)S(1)} %compare_convert_fusion.1.refs_0_.twice_ref, bf16[3,11,64,128]{3,2,1,0:T(8,128)(2,1)S(1)} %bitcast.63, ...), custom_call_target="tpu_custom_call" | custom-call | flops 1073741824 | bytes 419430400 | tf_op jit(solution)/shard_map/pallas_call | solution.py:269
  215.3 1.0 copy-done.3
  216.3 1.0 copy-done.5
  217.7 1.5 slice.40
  219.2 0.8 fusion.8
  219.9 0.4 copy.34
  220.3 1.0 broadcast_in_dim.108
  221.4 2.6 pad_maximum_fusion
  223.9 6.3 %all-to-all-start.2 = ((bf16[128,4,2176]{2,1,0:T(4,128)(2,1)}), bf16[128,4,2176]{2,1,0:T(4,128)(2,1)}, u32[]{:S(2)}, u32[]{:S(2)}) async-start(bf16[128,4,2176]{2,1,0:T(4,128)(2,1)} %bitcast.64), calls=%async_computation.2 | async-start | bytes 4456448 | tf_op jit(solution)/shard_map/all_to_all | solution.py:508
  230.3 1.2 copy-done.4
  231.5 29.0 %shard_map.157 = (bf16[24,8,2048]{2,1,0:T(8,128)(2,1)S(1)}, bf16[24,8,512]{2,1,0:T(8,128)(2,1)S(1)}) custom-call(s32[16]{0:T(128)S(1)} %compare_convert_fusion.1.refs_0_.twice_ref, f32[8,2048]{1,0:T(8,128)S(1)} %pad_convert_fusion.g_ref, bf16[3,11,32,4,64,128]{5,4,3,2,1,0:T(8,128)(2,1)} %bitcast.4.weight_ref, bf16[32,8,2048]{2,1,0:T(8,128)(2,1)S(1)} %copy-done.4, ...), custom_call_target="tpu_custom_call" | custom-call | flops 1073741824 | bytes 134217728 | tf_op jit(solution)/shard_map/pallas_call | solution.py:372
  261.2 0.7 fusion.10
  261.9 0.4 copy.42
  262.3 1.0 broadcast_in_dim.109
  263.3 2.5 pad_maximum_fusion.1
  265.9 10.2 %all-to-all-start.4 = ((bf16[128,4,2176]{2,1,0:T(4,128)(2,1)}), bf16[128,4,2176]{2,1,0:T(4,128)(2,1)}, u32[]{:S(2)}, u32[]{:S(2)}) async-start(bf16[128,4,2176]{2,1,0:T(4,128)(2,1)} %bitcast.65), calls=%async_computation.4 | async-start | bytes 4456448 | tf_op jit(solution)/shard_map/all_to_all | solution.py:508
  276.1 4.0 %reshape.165 = bf16[512,2176]{1,0:T(8,128)(2,1)} reshape(bf16[128,4,2176]{2,1,0:T(4,128)(2,1)} %all-to-all-done.2) | data formatting | bytes 4456448 | tf_op jit(solution)/shard_map/reshape | solution.py:509
  280.1 2.5 shard_map.156
  282.5 25.2 %all-to-all-done.4 = bf16[128,4,2176]{2,1,0:T(4,128)(2,1)} async-done(((bf16[128,4,2176]{2,1,0:T(4,128)(2,1)}), bf16[128,4,2176]{2,1,0:T(4,128)(2,1)}, u32[]{:S(2)}, u32[]{:S(2)}) %all-to-all-start.4) | async-done | bytes 2228256 | tf_op jit(solution)/shard_map/all_to_all | solution.py:508
  307.7 4.0 %all-to-all-start.3 = ((bf16[32,4,64,128]{3,2,1,0:T(8,128)(2,1)}), bf16[32,4,64,128]{3,2,1,0:T(8,128)(2,1)S(1)}, u32[]{:S(2)}, u32[]{:S(2)}) async-start(bf16[32,4,64,128]{3,2,1,0:T(8,128)(2,1)} %bitcast.18), calls=%async_computation.3 | async-start | bytes 4194304 | tf_op jit(solution)/shard_map/all_to_all | solution.py:466
  312.4 0.6 compare_reduce_fusion
  313.0 2.1 constant_dynamic-slice_fusion.3
  315.1 4.0 %reshape.170 = bf16[512,2176]{1,0:T(8,128)(2,1)} reshape(bf16[128,4,2176]{2,1,0:T(4,128)(2,1)} %all-to-all-done.4) | data formatting | bytes 4456448 | tf_op jit(solution)/shard_map/reshape | solution.py:509
  319.2 20.5 %all-to-all-done.3 = bf16[32,4,64,128]{3,2,1,0:T(8,128)(2,1)S(1)} async-done(((bf16[32,4,64,128]{3,2,1,0:T(8,128)(2,1)}), bf16[32,4,64,128]{3,2,1,0:T(8,128)(2,1)S(1)}, u32[]{:S(2)}, u32[]{:S(2)}) %all-to-all-start.3) | async-done | bytes 2097184 | tf_op jit(solution)/shard_map/all_to_all | solution.py:466
  339.6 0.5 convert_element_type.106
  340.2 0.9 slice_multiply_fusion
  341.1 0.7 copy-done.6
  341.8 0.7 copy-done.7
  342.5 3.1 fusion.5
  345.7 3.1 fusion.7
  (58 shorter events, 2.3 us)
Async XLA Ops:
  0.6 35.4 %copy-start = (bf16[128,2048]{1,0:T(8,128)(2,1)S(1)}, bf16[128,2048]{1,0:T(8,128)(2,1)}, u32[]{:S(2)}) copy-start(bf16[128,2048]{1,0:T(8,128)(2,1)} %param.11) | copy-start | bytes 1572868
  0.6 2.2 copy-start.12
  4.0 9.8 %copy-start.15 = (s32[24]{0:T(128)S(1)}, s32[24]{0:T(128)}, u32[]{:S(2)}) copy-start(s32[24]{0:T(128)} %param.19) | copy-start | bytes 292
  4.0 9.8 %copy-start.16 = (s32[16]{0:T(128)S(1)}, s32[16]{0:T(128)}, u32[]{:S(2)}) copy-start(s32[16]{0:T(128)} %param.20) | copy-start | bytes 196
  4.0 10.0 %copy-start.14 = (s32[24]{0:T(128)S(1)}, s32[24]{0:T(128)}, u32[]{:S(2)}) copy-start(s32[24]{0:T(128)} %param.21) | copy-start | bytes 292
  4.0 10.6 %copy-start.8 = (f32[1,2048,128]{2,1,0:T(8,128)S(1)}, f32[1,2048,128]{2,1,0:T(8,128)}, u32[]{:S(2)}) copy-start(f32[1,2048,128]{2,1,0:T(8,128)} %param.15) | copy-start | bytes 3145732
  5.1 25.8 %all-to-all-start = ((bf16[32,2,64,128]{3,2,1,0:T(8,128)(2,1)}), bf16[32,2,64,128]{3,2,1,0:T(8,128)(2,1)S(1)}, u32[]{:S(2)}, u32[]{:S(2)}) async-start(bf16[32,2,64,128]{3,2,1,0:T(8,128)(2,1)} %pad_maximum_fusion.3), calls=%async_computation | async-start | bytes 2097152 | tf_op jit(solution)/shard_map/all_to_all | solution.py:466
  13.8 1.2 copy-start.9
  13.8 1.5 copy-start.10
  14.6 1.4 copy-start.11
  30.8 1.0 copy-start.1
  31.8 192.1 %all-to-all-start.1 = ((bf16[32,4,64,128]{3,2,1,0:T(8,128)(2,1)}), bf16[32,4,64,128]{3,2,1,0:T(8,128)(2,1)S(1)}, u32[]{:S(2)}, u32[]{:S(2)}) async-start(bf16[32,4,64,128]{3,2,1,0:T(8,128)(2,1)} %pad_maximum_fusion.2), calls=%async_computation.1 | async-start | bytes 4194304 | tf_op jit(solution)/shard_map/all_to_all | solution.py:466
  36.9 1.2 copy-start.2
  215.3 1.0 copy-start.3
  216.3 1.0 copy-start.5
  223.9 41.9 %all-to-all-start.2 = ((bf16[128,4,2176]{2,1,0:T(4,128)(2,1)}), bf16[128,4,2176]{2,1,0:T(4,128)(2,1)}, u32[]{:S(2)}, u32[]{:S(2)}) async-start(bf16[128,4,2176]{2,1,0:T(4,128)(2,1)} %bitcast.64), calls=%async_computation.2 | async-start | bytes 4456448 | tf_op jit(solution)/shard_map/all_to_all | solution.py:508
  230.2 1.2 copy-start.4
  265.9 41.8 %all-to-all-start.4 = ((bf16[128,4,2176]{2,1,0:T(4,128)(2,1)}), bf16[128,4,2176]{2,1,0:T(4,128)(2,1)}, u32[]{:S(2)}, u32[]{:S(2)}) async-start(bf16[128,4,2176]{2,1,0:T(4,128)(2,1)} %bitcast.65), calls=%async_computation.4 | async-start | bytes 4456448 | tf_op jit(solution)/shard_map/all_to_all | solution.py:508
  307.7 31.9 %all-to-all-start.3 = ((bf16[32,4,64,128]{3,2,1,0:T(8,128)(2,1)}), bf16[32,4,64,128]{3,2,1,0:T(8,128)(2,1)S(1)}, u32[]{:S(2)}, u32[]{:S(2)}) async-start(bf16[32,4,64,128]{3,2,1,0:T(8,128)(2,1)} %bitcast.18), calls=%async_computation.3 | async-start | bytes 4194304 | tf_op jit(solution)/shard_map/all_to_all | solution.py:466
  340.1 1.6 copy-start.6
  340.1 2.3 copy-start.7
  340.1 2.4 copy-start.13
  342.5 3.1 slice-start

commit v5 on v4

--- a/solution.py
+++ b/solution.py
@@ -26,6 +26,15 @@
 
 def deep_of(units):
     return -(-units // groups)
+
+
+def folded(a):
+    half = a.shape[1] // 2
+    return (a[:, :half] + jnp.roll(a[:, half:], rows // 2, axis=0)).astype(bf16)
+
+
+def repeated(a):
+    return (a + jnp.roll(a, rows // 2, axis=0)).astype(bf16)
 
 
 def forward_layer(x, value, output):
@@ -176,9 +185,9 @@
         x = state[...]
         following, hidden, pre, units = forward_layer(x, wide(held[slot, 0]), wide(held[slot, 1]))
         in_ref[q] = x.astype(bf16)
-        hid_ref[q] = hidden
+        hid_ref[q] = folded(hidden.astype(f32))
         pre_ref[q] = pre
-        unit_ref[q] = units
+        unit_ref[q] = repeated(units.astype(f32))
         keep = jnp.maximum(twice_ref[layer], 1 - again) > 0
         state[...] = jnp.where(keep, following, x)
         return carry
@@ -273,7 +282,7 @@
         out_shape=[
             shape(own.shape[:2] + unit, bf16),
             shape((2 * old, rows, features), bf16),
-            shape((2 * old, rows, features), bf16),
+            shape((2 * old, rows, features // 2), bf16),
             shape((2 * old, rows, inner), f32),
             shape((2 * old, rows, inner), bf16),
         ],
@@ -349,8 +358,8 @@
             q = 2 * i + extra - r
             x = in_ref[q].astype(f32)
             g, gb, gz = backward_layer(x, pre_ref[q], state[...], wide(held[slot, 0]), wide(held[slot, 1]))
-            out_g_ref[j] = gb
-            out_z_ref[j] = gz
+            out_g_ref[j] = folded(gb.astype(f32))
+            out_z_ref[j] = repeated(gz.astype(f32))
             state[...] = g
             return j - 1
 
@@ -379,7 +388,10 @@
             vmem,
         ],
         out_specs=[vmem, vmem],
-        out_shape=[shape((new,) + a.shape[1:], bf16) for a in (saved_in, pre)],
+        out_shape=[
+            shape((new, rows, saved_in.shape[2] // 2), bf16),
+            shape((new, rows, pre.shape[2]), bf16),
+        ],
         scratch_shapes=[
             pltpu.VMEM((ahead, 2) + weights.shape[2:], bf16),
             pltpu.VMEM(g.shape, f32),
@@ -498,32 +510,34 @@
     send_layer = ((send_place[:, None] == places[None, :]) & holds[:, None]).astype(bf16)
 
     def message(choice, wide, narrow):
-        w = pick(choice, wide[:, :count])
-        n = pick(choice, narrow[:, :count])
-        n = n.reshape(sections, count, width, channels).transpose(0, 2, 1, 3)
-        w = jnp.broadcast_to(w[:, None], (sections, width, count, features))
-        return jnp.concatenate([w, n], axis=-1).reshape(sections * width, count, features + channels)
-
-    def to_owner(sent):
-        got = lax.all_to_all(sent, both, split_axis=0, concat_axis=0, tiled=True)
-        got = got.reshape(sections * width * count, features + channels)
-        return got[:, :features], got[:, features:]
-
-    forward_sent = message(send_layer, hidden, units)
+        w = pick(choice, wide)
+        n = pick(choice, narrow)
+        n = n.reshape(sections, rows, width, channels).transpose(0, 2, 1, 3)
+        w = jnp.broadcast_to(w[:, None], (sections, width) + w.shape[1:])
+        return [w, n]
+
     entering = mine(cotangent)
-    forward_sent, moments, entering = lax.optimization_barrier((forward_sent, moments, entering))
-    hidden_all, units_all = to_owner(forward_sent)
+    moments, saved_in = lax.optimization_barrier((moments, saved_in))
+    moments = pick_slots(wanted, holds.astype(jnp.int32), moments)
+    moments, entering = lax.optimization_barrier((moments, entering))
+    moments = spread(moments)
     grads, inner_grads = run_backward(new, twice, entering, gathered, saved_in, pre)
-    grads_all, inner_all = to_owner(message(owner_match.astype(bf16), grads, inner_grads))
-    moments, hidden_all = lax.optimization_barrier((moments, hidden_all))
-    moments = pick_slots(wanted, holds.astype(jnp.int32), moments)
-    moments = spread(moments)
+    sent = message(send_layer, hidden, units) + message(owner_match.astype(bf16), grads, inner_grads)
+    sent = jnp.concatenate(sent, axis=-1)
+    sent = sent.reshape((sections * width,) + sent.shape[2:])
+    got = lax.all_to_all(sent, both, split_axis=0, concat_axis=0, tiled=True)
+    got = got.reshape(sections * width * rows, got.shape[-1])
+    fold = features // 2
+    low = (lax.broadcasted_iota(jnp.int32, (got.shape[0], 1), 0) % rows) < rows // 2
 
     def weight_grad(a, b):
-        return lax.dot_general(a, b, (((0,), (0,)), ((), ())), preferred_element_type=f32)
-
-    grad_value = weight_grad(hidden_all, inner_all)
-    grad_output = weight_grad(grads_all, units_all)
+        b = jnp.concatenate([jnp.where(low, b, 0), jnp.where(low, 0, b)], axis=1)
+        g = lax.dot_general(a, b, (((0,), (0,)), ((), ())), preferred_element_type=f32)
+        return jnp.concatenate([g[:, :channels], g[:, channels:]], axis=0)
+
+    grad_value = weight_grad(got[:, :fold], got[:, 2 * fold + channels :])
+    grad_output = weight_grad(got[:, fold + channels : 2 * fold + channels], got[:, fold : fold + channels])
+
     def own_of(which):
         unit = 2 * my_old + which
         got = lax.dynamic_slice(

time: 351 us -> 343 us (0.977)
  local copies, waits for them, and re-layouts: 27.2 us -> 16.4 us
  other arithmetic: 12.3 us -> 21.8 us
  starting transfers between devices: 33.1 us -> 26.9 us
  waiting for transfers between devices: 57.5 us -> 61.7 us
    all_to_all x2 -> x1, waiting for transfers between devices: 25.2 us -> 51 us  [body(): got = lax.all_to_all(sent, both, split_axis=0, concat_axis=0, tiled=True)]
    all_to_all x3, waiting for transfers between devices: 32.3 us -> 10.7 us  [spread(): return lax.all_to_all(a, section, split_axis=0, concat_axis=0, tiled=True)]
    all_to_all x2 -> x1, starting transfers between devices: 16.4 us -> 8.28 us  [body(): got = lax.all_to_all(sent, both, split_axis=0, concat_axis=0, tiled=True)]
    reshape x4 -> x2, local copies, waits for them, and re-layouts: 8.14 us -> 0.14 us  [message(): n = n.reshape(sections, rows, width, channels).transpose(0, 2, 1, 3)]
    convert_element_type x0 -> x1, other arithmetic: none -> 3.79 us  [adam_update(): weight_new = jnp.where(owned, weight_new, 0.0).astype(bf16)]
    unnamed x34 -> x30, local copies, waits for them, and re-layouts: 8.06 us -> 5.35 us
  transfers between devices with their start and end apart: 5 -> 4, of which waited for: 3 -> 2; matrix products, arithmetic and copies ran while one was open for 8% -> 7% of each run, Pallas kernels for 60% -> 60%
where the time goes in v5:
time: 343 us; the launch traced here: 342 us
  Pallas kernels  206 us (60%)
  waiting for transfers between devices  61.7 us (18%)
  starting transfers between devices  26.9 us (8%)
  other arithmetic  21.8 us (6%)
  local copies, waits for them, and re-layouts  16.4 us (5%)
  matrix products  7.69 us (2%)
    pallas_call x1, Pallas kernels, gather_forward(): pl.pallas_call(lambda *refs: gather_kernel(old, *refs), in_specs=[pl.Bloc...  174 us
    all_to_all x1, waiting for transfers between devices, body(): got = lax.all_to_all(sent, both, split_axis=0, concat_axis=0, tiled=True)  51 us
    pallas_call x1, Pallas kernels, run_backward(): pl.pallas_call(backward_kernel, in_specs=[pl.BlockSpec(memory_space=pltpu...  29.4 us
    all_to_all x3, starting transfers between devices, spread(): return lax.all_to_all(a, section, split_axis=0, concat_axis=0, tiled=True)  18.7 us
    all_to_all x3, waiting for transfers between devices, spread(): return lax.all_to_all(a, section, split_axis=0, concat_axis=0, tiled=True)  10.7 us
    all_to_all x1, starting transfers between devices, body(): got = lax.all_to_all(sent, both, split_axis=0, concat_axis=0, tiled=True)  8.28 us
  transfers between devices with their start and end apart: 4, of which 2 were waited for; matrix products, arithmetic and copies ran while one was open for 7% of the time, Pallas kernels for 60%

profile of v5, /device:TPU:1, one launch (start us, length us, event | category | flops | bytes accessed | tf_op | source)
XLA Modules:
  0.0 342.0 jit_solution(8399846019246501800)
XLA Ops:
  0.6 1.2 reshape.509
  1.9 0.5 copy.31
  2.4 0.4 stack_reshape.6
  2.8 1.2 reshape.510
  4.0 0.5 copy.32
  4.6 0.4 stack_reshape.7
  5.0 1.1 pad_maximum_fusion.2
  6.0 8.7 %all-to-all-start = ((bf16[32,2,64,128]{3,2,1,0:T(8,128)(2,1)}), bf16[32,2,64,128]{3,2,1,0:T(8,128)(2,1)S(1)}, u32[]{:S(2)}, u32[]{:S(2)}) async-start(bf16[32,2,64,128]{3,2,1,0:T(8,128)(2,1)} %pad_maximum_fusion.2), calls=%async_computation | async-start | bytes 2097152 | tf_op jit(solution)/shard_map/all_to_all | solution.py:478
  14.9 1.4 convert_element_type.133
  16.3 1.3 convert_element_type.135
  17.6 0.8 convert_element_type.137
  18.6 2.7 pad_maximum_fusion.1
  21.2 10.7 %all-to-all-done = bf16[32,2,64,128]{3,2,1,0:T(8,128)(2,1)S(1)} async-done(((bf16[32,2,64,128]{3,2,1,0:T(8,128)(2,1)}), bf16[32,2,64,128]{3,2,1,0:T(8,128)(2,1)S(1)}, u32[]{:S(2)}, u32[]{:S(2)}) %all-to-all-start) | async-done | bytes 1048608 | tf_op jit(solution)/shard_map/all_to_all | solution.py:478
  31.9 1.0 copy-done.2
  32.9 4.1 %all-to-all-start.1 = ((bf16[32,4,64,128]{3,2,1,0:T(8,128)(2,1)}), bf16[32,4,64,128]{3,2,1,0:T(8,128)(2,1)S(1)}, u32[]{:S(2)}, u32[]{:S(2)}) async-start(bf16[32,4,64,128]{3,2,1,0:T(8,128)(2,1)} %pad_maximum_fusion.1), calls=%async_computation.1 | async-start | bytes 4194304 | tf_op jit(solution)/shard_map/all_to_all | solution.py:478
  37.0 0.6 fusion.43
  37.8 1.3 fusion.45
  39.3 0.8 constant_dynamic-slice_fusion
  40.1 1.2 copy-done.3
  41.3 1.0 shard_map.154
  42.3 174.1 %shard_map.155 = (bf16[3,11,2,4,4,4,64,128]{7,6,5,4,3,2,1,0:T(8,128)(2,1)}, bf16[32,8,2048]{2,1,0:T(8,128)(2,1)S(1)}, bf16[32,8,1024]{2,1,0:T(8,128)(2,1)S(1)}, ...) custom-call(s32[16]{0:T(128)S(1)} %compare_convert_fusion.1.refs_0_.twice_ref, bf16[3,11,64,128]{3,2,1,0:T(8,128)(2,1)S(1)} %bitcast.57, ...), custom_call_target="tpu_custom_call" | custom-call | flops 1073741824 | bytes 419430400 | tf_op jit(solution)/shard_map/pallas_call | solution.py:278
  216.4 1.0 copy-done.4
  217.4 0.8 copy-done.6
  218.2 1.1 shard_map.156
  219.3 1.3 copy-done.1
  220.7 5.9 %all-to-all-start.2 = ((bf16[32,4,64,128]{3,2,1,0:T(8,128)(2,1)}), bf16[32,4,64,128]{3,2,1,0:T(8,128)(2,1)}, u32[]{:S(2)}, u32[]{:S(2)}) async-start(bf16[32,4,64,128]{3,2,1,0:T(8,128)(2,1)} %bitcast.55), calls=%async_computation.2 | async-start | bytes 4194304 | tf_op jit(solution)/shard_map/all_to_all | solution.py:478
  226.6 1.8 fusion.16
  228.4 1.1 copy.38
  229.5 0.3 fusion.20
  229.8 0.3 copy.43
  230.1 29.4 %shard_map.157 = (bf16[24,8,1024]{2,1,0:T(8,128)(2,1)S(1)}, bf16[24,8,512]{2,1,0:T(8,128)(2,1)S(1)}) custom-call(s32[16]{0:T(128)S(1)} %compare_convert_fusion.1.refs_0_.twice_ref, f32[8,2048]{1,0:T(8,128)S(1)} %pad_convert_fusion.g_ref, bf16[3,11,32,4,64,128]{5,4,3,2,1,0:T(8,128)(2,1)} %bitcast.4.weight_ref, bf16[32,8,2048]{2,1,0:T(8,128)(2,1)S(1)} %copy-done.5, ...), custom_call_target="tpu_custom_call" | custom-call | flops 1073741824 | bytes 134217728 | tf_op jit(solution)/shard_map/pallas_call | solution.py:381
  259.5 0.5 fusion.18
  260.0 0.3 copy.41
  260.3 0.3 fusion.22
  260.7 0.3 copy.44
  261.0 1.3 broadcast_in_dim.130
  262.3 0.3 broadcast_in_dim.131
  262.6 2.5 pad_maximum_fusion
  265.1 8.3 %all-to-all-start.3 = ((bf16[128,8,2304]{2,1,0:T(8,128)(2,1)}), bf16[128,8,2304]{2,1,0:T(8,128)(2,1)}, u32[]{:S(2)}, u32[]{:S(2)}) async-start(bf16[128,8,2304]{2,1,0:T(8,128)(2,1)} %bitcast.58), calls=%async_computation.3 | async-start | bytes 9437184 | tf_op jit(solution)/shard_map/all_to_all | solution.py:528
  274.1 0.6 compare_reduce_fusion
  274.7 2.1 constant_dynamic-slice_fusion.3
  276.8 2.1 convert_element_type.139
  278.8 2.0 slice_multiply_fusion
  280.9 51.0 %all-to-all-done.3 = bf16[128,8,2304]{2,1,0:T(8,128)(2,1)} async-done(((bf16[128,8,2304]{2,1,0:T(8,128)(2,1)}), bf16[128,8,2304]{2,1,0:T(8,128)(2,1)}, u32[]{:S(2)}, u32[]{:S(2)}) %all-to-all-start.3) | async-done | bytes 4718624 | tf_op jit(solution)/shard_map/all_to_all | solution.py:528
  331.9 1.2 broadcast_select_fusion.1
  333.1 2.3 fusion.2
  335.6 2.5 fusion
  338.2 3.8 %fusion.7 = (bf16[1,2048,128]{2,1,0:T(8,128)(2,1)}, f32[1,2048,128]{2,1,0:T(8,128)}, f32[1,2048,128]{2,1,0:T(8,128)}, bf16[1,2048,128]{2,1,0:T(8,128)(2,1)}, f32...) fusion(bf16[1,1,32,1,64,128]{5,4,3,2,1,0:T(8,128)(2,1)S(1)} %get-tuple-element.38, pred[]{:T(512)} %compare_reduce_fusion, ...), kind=kLoop, calls=%fused_computation.19 | loop fusion | flops 6815744 | bytes 12582913 | tf_op jit(solution)/shard_map/convert_element_type | solution.py:440
  (48 shorter events, 1.0 us)
Async XLA Ops:
  0.6 38.6 %copy-start = (bf16[128,2048]{1,0:T(8,128)(2,1)S(1)}, bf16[128,2048]{1,0:T(8,128)(2,1)}, u32[]{:S(2)}) copy-start(bf16[128,2048]{1,0:T(8,128)(2,1)} %param.11) | copy-start | bytes 1572868
  1.9 13.0 %copy-start.10 = (f32[1,2048,128]{2,1,0:T(8,128)S(1)}, f32[1,2048,128]{2,1,0:T(8,128)}, u32[]{:S(2)}) copy-start(f32[1,2048,128]{2,1,0:T(8,128)} %param.15) | copy-start | bytes 3145732
  6.0 12.4 %copy-start.13 = (s32[24]{0:T(128)S(1)}, s32[24]{0:T(128)}, u32[]{:S(2)}) copy-start(s32[24]{0:T(128)} %param.21) | copy-start | bytes 292
  6.0 25.9 %all-to-all-start = ((bf16[32,2,64,128]{3,2,1,0:T(8,128)(2,1)}), bf16[32,2,64,128]{3,2,1,0:T(8,128)(2,1)S(1)}, u32[]{:S(2)}, u32[]{:S(2)}) async-start(bf16[32,2,64,128]{3,2,1,0:T(8,128)(2,1)} %pad_maximum_fusion.2), calls=%async_computation | async-start | bytes 2097152 | tf_op jit(solution)/shard_map/all_to_all | solution.py:478
  14.9 2.7 copy-start.11
  17.6 20.0 %copy-start.12 = (s32[24]{0:T(128)S(1)}, s32[24]{0:T(128)}, u32[]{:S(2)}) copy-start(s32[24]{0:T(128)} %param.19) | copy-start | bytes 292
  17.6 20.0 %copy-start.14 = (s32[16]{0:T(128)S(1)}, s32[16]{0:T(128)}, u32[]{:S(2)}) copy-start(s32[16]{0:T(128)} %param.20) | copy-start | bytes 196
  31.9 1.0 copy-start.2
  32.9 185.3 %all-to-all-start.1 = ((bf16[32,4,64,128]{3,2,1,0:T(8,128)(2,1)}), bf16[32,4,64,128]{3,2,1,0:T(8,128)(2,1)S(1)}, u32[]{:S(2)}, u32[]{:S(2)}) async-start(bf16[32,4,64,128]{3,2,1,0:T(8,128)(2,1)} %pad_maximum_fusion.1), calls=%async_computation.1 | async-start | bytes 4194304 | tf_op jit(solution)/shard_map/all_to_all | solution.py:478
  40.1 1.2 copy-start.3
  216.4 1.0 copy-start.4
  217.4 0.8 copy-start.6
  219.3 1.4 copy-start.1
  220.7 9.4 %copy-start.5 = (bf16[32,8,2048]{2,1,0:T(8,128)(2,1)S(1)}, bf16[32,8,2048]{2,1,0:T(8,128)(2,1)}, u32[]{:S(2)}) copy-start(bf16[32,8,2048]{2,1,0:T(8,128)(2,1)} %copy-done.4) | copy-start | bytes 3145732
  220.7 44.4 %all-to-all-start.2 = ((bf16[32,4,64,128]{3,2,1,0:T(8,128)(2,1)}), bf16[32,4,64,128]{3,2,1,0:T(8,128)(2,1)}, u32[]{:S(2)}, u32[]{:S(2)}) async-start(bf16[32,4,64,128]{3,2,1,0:T(8,128)(2,1)} %bitcast.55), calls=%async_computation.2 | async-start | bytes 4194304 | tf_op jit(solution)/shard_map/all_to_all | solution.py:478
  265.1 66.8 %all-to-all-start.3 = ((bf16[128,8,2304]{2,1,0:T(8,128)(2,1)}), bf16[128,8,2304]{2,1,0:T(8,128)(2,1)}, u32[]{:S(2)}, u32[]{:S(2)}) async-start(bf16[128,8,2304]{2,1,0:T(8,128)(2,1)} %bitcast.58), calls=%async_computation.3 | async-start | bytes 9437184 | tf_op jit(solution)/shard_map/all_to_all | solution.py:528
  335.5 2.6 copy-start.7
  335.6 2.6 copy-start.8
  335.6 2.6 copy-start.9

commit v6 on v5

--- a/solution.py
+++ b/solution.py
@@ -233,6 +233,14 @@
     spread_start(3)
     plane_start(1)
 
+    def drain(k):
+        for g in range(groups):
+            for phase in (1, 2):
+                for c in first(g, phase, k) + second(g, phase, k):
+                    c.wait_send()
+            for c in cross(g, k):
+                c.wait_send()
+
     def step(t, carry):
         def at(k, act):
             @pl.when((k >= 0) & (k < deep))
@@ -245,25 +253,19 @@
         at(t + 4, spread_start)
         at(t - 1, cross_start)
         at(t - 2, use)
+        at(t - 3, drain)
+
+        @pl.when(t == 1)
+        def _():
+            for g in range(groups):
+                for b in range(2):
+                    for c in bulk_first(g, b) + bulk_second(g, b):
+                        c.wait_send()
+
         return carry
 
     lax.fori_loop(0, deep + 2, step, 0)
-
-    for g in range(groups):
-        for b in range(2):
-            for c in bulk_first(g, b) + bulk_second(g, b):
-                c.wait_send()
-
-    def drain(k, carry):
-        for g in range(groups):
-            for phase in (1, 2):
-                for c in first(g, phase, k) + second(g, phase, k):
-                    c.wait_send()
-            for c in cross(g, k):
-                c.wait_send()
-        return carry
-
-    lax.fori_loop(0, deep, drain, 0)
+    drain(deep - 1)
 
 
 def gather_forward(twice, own, x):
@@ -478,7 +480,7 @@
         return lax.all_to_all(a, section, split_axis=0, concat_axis=0, tiled=True)
 
     def turned(a):
-        return a.reshape(2, ring, ring, part * channels).transpose(2, 1, 0, 3)
+        return a.reshape(2, ring, ring, part, channels).transpose(2, 1, 0, 3, 4)
 
     old = old_section.shape[0]
     pieces = spread(pieces_of((turned(value_weight), turned(output_weight))))
@@ -488,7 +490,6 @@
     ).reshape(-1)
     unit_match = (unit // 2)[:, None] == lax.iota(jnp.int32, old)[None, :]
     slots = 2 * jnp.sum(jnp.where(unit_match, old_section[None, :], 0), axis=1) + unit % 2
-    own = pick_slots(slots, jnp.ones_like(slots), pieces.reshape(2 * sections, part, channels))
     count = tokens.shape[0] // sections
 
     def mine(a):
@@ -499,8 +500,10 @@
     twice = (jnp.sum((layer_map[:, None] == numbers[None, :]).astype(jnp.int32), axis=0) > 1).astype(jnp.int32)
     before = jnp.concatenate([jnp.full((1,), -1, jnp.int32), layer_map[:-1]])
     place_of = 2 * layer_map + (before == layer_map).astype(jnp.int32)
+    pieces, slots, twice, starting = lax.optimization_barrier((pieces, slots, twice, mine(tokens)))
+    own = pick_slots(slots, jnp.ones_like(slots), pieces.reshape(2 * sections, part, channels))
     gathered, saved_in, hidden, pre, units = gather_forward(
-        twice, own.reshape(groups, deep, part, channels), mine(tokens)
+        twice, own.reshape(groups, deep, part, channels), starting
     )
     gathered = gathered.reshape(groups, deep, sections, width, part, channels)
     moments = spread(pieces_of((value_first, output_first, value_second, output_second)))

time: 343 us -> 341 us (level)
  no operation moved by 1% of the time
where the time goes in v6:
time: 341 us; the launch traced here: 340 us
  Pallas kernels  205 us (60%)
  waiting for transfers between devices  61.7 us (18%)
  starting transfers between devices  27.1 us (8%)
  other arithmetic  21.8 us (6%)
  local copies, waits for them, and re-layouts  14.4 us (4%)
  matrix products  7.7 us (2%)
    pallas_call x1, Pallas kernels, gather_forward(): pl.pallas_call(lambda *refs: gather_kernel(old, *refs), in_specs=[pl.Bloc...  174 us
    all_to_all x1, waiting for transfers between devices, body(): got = lax.all_to_all(sent, both, split_axis=0, concat_axis=0, tiled=True)  51 us
    pallas_call x1, Pallas kernels, run_backward(): pl.pallas_call(backward_kernel, in_specs=[pl.BlockSpec(memory_space=pltpu...  29.1 us
    all_to_all x3, starting transfers between devices, spread(): return lax.all_to_all(a, section, split_axis=0, concat_axis=0, tiled=True)  18.7 us
    all_to_all x3, waiting for transfers between devices, spread(): return lax.all_to_all(a, section, split_axis=0, concat_axis=0, tiled=True)  10.7 us
    all_to_all x1, starting transfers between devices, body(): got = lax.all_to_all(sent, both, split_axis=0, concat_axis=0, tiled=True)  8.45 us
  transfers between devices with their start and end apart: 4, of which 2 were waited for; matrix products, arithmetic and copies ran while one was open for 7% of the time, Pallas kernels for 60%

profile of v6, /device:TPU:1, one launch (start us, length us, event | category | flops | bytes accessed | tf_op | source)
XLA Modules:
  0.0 339.6 jit_solution(6691345980394742953)
XLA Ops:
  0.7 1.2 copy.31
  1.9 1.1 copy.32
  2.9 1.1 pad_maximum_fusion.2
  4.0 8.7 %all-to-all-start = ((bf16[32,2,64,128]{3,2,1,0:T(8,128)(2,1)}), bf16[32,2,64,128]{3,2,1,0:T(8,128)(2,1)S(1)}, u32[]{:S(2)}, u32[]{:S(2)}) async-start(bf16[32,2,64,128]{3,2,1,0:T(8,128)(2,1)} %pad_maximum_fusion.2), calls=%async_computation | async-start | bytes 2097152 | tf_op jit(solution)/shard_map/all_to_all | solution.py:480
  12.9 1.4 convert_element_type.133
  14.3 1.3 convert_element_type.135
  15.6 0.8 convert_element_type.137
  16.4 0.1 fusion.29
  16.5 2.7 pad_maximum_fusion.1
  19.2 10.7 %all-to-all-done = bf16[32,2,64,128]{3,2,1,0:T(8,128)(2,1)S(1)} async-done(((bf16[32,2,64,128]{3,2,1,0:T(8,128)(2,1)}), bf16[32,2,64,128]{3,2,1,0:T(8,128)(2,1)S(1)}, u32[]{:S(2)}, u32[]{:S(2)}) %all-to-all-start) | async-done | bytes 1048608 | tf_op jit(solution)/shard_map/all_to_all | solution.py:480
  29.9 1.0 copy-done.2
  30.9 4.1 %all-to-all-start.1 = ((bf16[32,4,64,128]{3,2,1,0:T(8,128)(2,1)}), bf16[32,4,64,128]{3,2,1,0:T(8,128)(2,1)S(1)}, u32[]{:S(2)}, u32[]{:S(2)}) async-start(bf16[32,4,64,128]{3,2,1,0:T(8,128)(2,1)} %pad_maximum_fusion.1), calls=%async_computation.1 | async-start | bytes 4194304 | tf_op jit(solution)/shard_map/all_to_all | solution.py:480
  35.0 0.6 fusion.43
  35.6 0.1 convert_reduce_fusion
  35.7 0.1 select_reduce_fusion.3
  35.8 1.3 fusion.45
  37.1 0.1 select_reduce_fusion
  37.2 0.8 constant_dynamic-slice_fusion
  38.1 1.2 copy-done.3
  39.3 1.0 shard_map.154
  40.3 173.9 %shard_map.155 = (bf16[3,11,2,4,4,4,64,128]{7,6,5,4,3,2,1,0:T(8,128)(2,1)}, bf16[32,8,2048]{2,1,0:T(8,128)(2,1)S(1)}, bf16[32,8,1024]{2,1,0:T(8,128)(2,1)S(1)}, ...) custom-call(s32[16]{0:T(128)S(1)} %compare_convert_fusion.1.refs_0_.twice_ref, bf16[3,11,64,128]{3,2,1,0:T(8,128)(2,1)S(1)} %bitcast.63, ...), custom_call_target="tpu_custom_call" | custom-call | flops 1073741824 | bytes 419430400 | tf_op jit(solution)/shard_map/pallas_call | solution.py:280
  214.2 1.0 copy-done.4
  215.2 0.8 copy-done.6
  216.0 1.1 shard_map.156
  217.1 1.3 copy-done.1
  218.4 5.9 %all-to-all-start.2 = ((bf16[32,4,64,128]{3,2,1,0:T(8,128)(2,1)}), bf16[32,4,64,128]{3,2,1,0:T(8,128)(2,1)}, u32[]{:S(2)}, u32[]{:S(2)}) async-start(bf16[32,4,64,128]{3,2,1,0:T(8,128)(2,1)} %bitcast.61), calls=%async_computation.2 | async-start | bytes 4194304 | tf_op jit(solution)/shard_map/all_to_all | solution.py:480
  224.3 1.8 fusion.16
  226.1 1.1 copy.38
  227.2 0.3 fusion.20
  227.6 0.3 copy.43
  227.9 29.1 %shard_map.157 = (bf16[24,8,1024]{2,1,0:T(8,128)(2,1)S(1)}, bf16[24,8,512]{2,1,0:T(8,128)(2,1)S(1)}) custom-call(s32[16]{0:T(128)S(1)} %compare_convert_fusion.1.refs_0_.twice_ref, f32[8,2048]{1,0:T(8,128)S(1)} %pad_convert_fusion.g_ref, bf16[3,11,32,4,64,128]{5,4,3,2,1,0:T(8,128)(2,1)} %bitcast.8.weight_ref, bf16[32,8,2048]{2,1,0:T(8,128)(2,1)S(1)} %copy-done.5, ...), custom_call_target="tpu_custom_call" | custom-call | flops 1073741824 | bytes 134217728 | tf_op jit(solution)/shard_map/pallas_call | solution.py:383
  257.0 0.5 fusion.18
  257.4 0.3 copy.41
  257.7 0.3 fusion.22
  258.2 0.3 copy.44
  258.5 1.3 broadcast_in_dim.130
  259.8 0.3 broadcast_in_dim.131
  260.0 2.5 pad_maximum_fusion
  262.5 8.4 %all-to-all-start.3 = ((bf16[128,8,2304]{2,1,0:T(8,128)(2,1)}), bf16[128,8,2304]{2,1,0:T(8,128)(2,1)}, u32[]{:S(2)}, u32[]{:S(2)}) async-start(bf16[128,8,2304]{2,1,0:T(8,128)(2,1)} %bitcast.64), calls=%async_computation.3 | async-start | bytes 9437184 | tf_op jit(solution)/shard_map/all_to_all | solution.py:531
  271.7 0.6 compare_reduce_fusion
  272.3 2.1 constant_dynamic-slice_fusion.3
  274.4 2.1 convert_element_type.139
  276.5 2.0 slice_multiply_fusion
  278.5 51.0 %all-to-all-done.3 = bf16[128,8,2304]{2,1,0:T(8,128)(2,1)} async-done(((bf16[128,8,2304]{2,1,0:T(8,128)(2,1)}), bf16[128,8,2304]{2,1,0:T(8,128)(2,1)}, u32[]{:S(2)}, u32[]{:S(2)}) %all-to-all-start.3) | async-done | bytes 4718624 | tf_op jit(solution)/shard_map/all_to_all | solution.py:531
  329.5 1.2 broadcast_select_fusion.1
  330.7 2.3 fusion.2
  333.2 2.5 fusion
  335.8 3.8 %fusion.7 = (bf16[1,2048,128]{2,1,0:T(8,128)(2,1)}, f32[1,2048,128]{2,1,0:T(8,128)}, f32[1,2048,128]{2,1,0:T(8,128)}, bf16[1,2048,128]{2,1,0:T(8,128)(2,1)}, f32...) fusion(bf16[1,1,32,1,64,128]{5,4,3,2,1,0:T(8,128)(2,1)S(1)} %get-tuple-element.46, pred[]{:T(512)} %compare_reduce_fusion, ...), kind=kLoop, calls=%fused_computation.19 | loop fusion | flops 6815744 | bytes 12582913 | tf_op jit(solution)/shard_map/convert_element_type | solution.py:442
  (44 shorter events, 0.6 us)
Async XLA Ops:
  0.6 36.6 %copy-start = (bf16[128,2048]{1,0:T(8,128)(2,1)S(1)}, bf16[128,2048]{1,0:T(8,128)(2,1)}, u32[]{:S(2)}) copy-start(bf16[128,2048]{1,0:T(8,128)(2,1)} %param.11) | copy-start | bytes 1572868
  0.6 12.2 %copy-start.10 = (f32[1,2048,128]{2,1,0:T(8,128)S(1)}, f32[1,2048,128]{2,1,0:T(8,128)}, u32[]{:S(2)}) copy-start(f32[1,2048,128]{2,1,0:T(8,128)} %param.15) | copy-start | bytes 3145732
  4.0 12.4 %copy-start.13 = (s32[24]{0:T(128)S(1)}, s32[24]{0:T(128)}, u32[]{:S(2)}) copy-start(s32[24]{0:T(128)} %param.21) | copy-start | bytes 292
  4.0 25.9 %all-to-all-start = ((bf16[32,2,64,128]{3,2,1,0:T(8,128)(2,1)}), bf16[32,2,64,128]{3,2,1,0:T(8,128)(2,1)S(1)}, u32[]{:S(2)}, u32[]{:S(2)}) async-start(bf16[32,2,64,128]{3,2,1,0:T(8,128)(2,1)} %pad_maximum_fusion.2), calls=%async_computation | async-start | bytes 2097152 | tf_op jit(solution)/shard_map/all_to_all | solution.py:480
  12.9 2.7 copy-start.11
  15.6 20.0 %copy-start.12 = (s32[24]{0:T(128)S(1)}, s32[24]{0:T(128)}, u32[]{:S(2)}) copy-start(s32[24]{0:T(128)} %param.19) | copy-start | bytes 292
  15.6 20.0 %copy-start.14 = (s32[16]{0:T(128)S(1)}, s32[16]{0:T(128)}, u32[]{:S(2)}) copy-start(s32[16]{0:T(128)} %param.20) | copy-start | bytes 196
  29.9 1.0 copy-start.2
  30.9 185.1 %all-to-all-start.1 = ((bf16[32,4,64,128]{3,2,1,0:T(8,128)(2,1)}), bf16[32,4,64,128]{3,2,1,0:T(8,128)(2,1)S(1)}, u32[]{:S(2)}, u32[]{:S(2)}) async-start(bf16[32,4,64,128]{3,2,1,0:T(8,128)(2,1)} %pad_maximum_fusion.1), calls=%async_computation.1 | async-start | bytes 4194304 | tf_op jit(solution)/shard_map/all_to_all | solution.py:480
  38.1 1.2 copy-start.3
  214.2 1.0 copy-start.4
  215.2 0.8 copy-start.6
  217.1 1.4 copy-start.1
  218.4 9.4 %copy-start.5 = (bf16[32,8,2048]{2,1,0:T(8,128)(2,1)S(1)}, bf16[32,8,2048]{2,1,0:T(8,128)(2,1)}, u32[]{:S(2)}) copy-start(bf16[32,8,2048]{2,1,0:T(8,128)(2,1)} %copy-done.4) | copy-start | bytes 3145732
  218.4 44.0 %all-to-all-start.2 = ((bf16[32,4,64,128]{3,2,1,0:T(8,128)(2,1)}), bf16[32,4,64,128]{3,2,1,0:T(8,128)(2,1)}, u32[]{:S(2)}, u32[]{:S(2)}) async-start(bf16[32,4,64,128]{3,2,1,0:T(8,128)(2,1)} %bitcast.61), calls=%async_computation.2 | async-start | bytes 4194304 | tf_op jit(solution)/shard_map/all_to_all | solution.py:480
  262.5 67.0 %all-to-all-start.3 = ((bf16[128,8,2304]{2,1,0:T(8,128)(2,1)}), bf16[128,8,2304]{2,1,0:T(8,128)(2,1)}, u32[]{:S(2)}, u32[]{:S(2)}) async-start(bf16[128,8,2304]{2,1,0:T(8,128)(2,1)} %bitcast.64), calls=%async_computation.3 | async-start | bytes 9437184 | tf_op jit(solution)/shard_map/all_to_all | solution.py:531
  333.1 2.6 copy-start.7
  333.2 2.6 copy-start.8
  333.2 2.6 copy-start.9

commit v7 on v6

--- a/solution.py
+++ b/solution.py
@@ -247,11 +247,11 @@
             def _():
                 act(k)
 
+        at(t - 1, cross_start)
         at(t, plane_pass)
         at(t + 2, plane_start)
         at(t + 3, spread_pass)
         at(t + 4, spread_start)
-        at(t - 1, cross_start)
         at(t - 2, use)
         at(t - 3, drain)
 

time: 341 us -> 341 us (level)
  no operation moved by 1% of the time
where the time goes in v7:
time: 341 us; the launch traced here: 340 us
  Pallas kernels  205 us (60%)
  waiting for transfers between devices  61.7 us (18%)
  starting transfers between devices  27.2 us (8%)
  other arithmetic  21.8 us (6%)
  local copies, waits for them, and re-layouts  14.4 us (4%)
  matrix products  7.7 us (2%)
    pallas_call x1, Pallas kernels, gather_forward(): pl.pallas_call(lambda *refs: gather_kernel(old, *refs), in_specs=[pl.Bloc...  174 us
    all_to_all x1, waiting for transfers between devices, body(): got = lax.all_to_all(sent, both, split_axis=0, concat_axis=0, tiled=True)  51 us
    pallas_call x1, Pallas kernels, run_backward(): pl.pallas_call(backward_kernel, in_specs=[pl.BlockSpec(memory_space=pltpu...  29.2 us
    all_to_all x3, starting transfers between devices, spread(): return lax.all_to_all(a, section, split_axis=0, concat_axis=0, tiled=True)  18.7 us
    all_to_all x3, waiting for transfers between devices, spread(): return lax.all_to_all(a, section, split_axis=0, concat_axis=0, tiled=True)  10.7 us
    all_to_all x1, starting transfers between devices, body(): got = lax.all_to_all(sent, both, split_axis=0, concat_axis=0, tiled=True)  8.54 us
  transfers between devices with their start and end apart: 4, of which 2 were waited for; matrix products, arithmetic and copies ran while one was open for 7% of the time, Pallas kernels for 60%

profile of v7, /device:TPU:1, one launch (start us, length us, event | category | flops | bytes accessed | tf_op | source)
XLA Modules:
  0.0 340.0 jit_solution(11229026667833742642)
XLA Ops:
  0.7 1.2 copy.31
  1.9 1.1 copy.32
  2.9 1.1 pad_maximum_fusion.2
  4.0 8.7 %all-to-all-start = ((bf16[32,2,64,128]{3,2,1,0:T(8,128)(2,1)}), bf16[32,2,64,128]{3,2,1,0:T(8,128)(2,1)S(1)}, u32[]{:S(2)}, u32[]{:S(2)}) async-start(bf16[32,2,64,128]{3,2,1,0:T(8,128)(2,1)} %pad_maximum_fusion.2), calls=%async_computation | async-start | bytes 2097152 | tf_op jit(solution)/shard_map/all_to_all | solution.py:480
  12.9 1.4 convert_element_type.133
  14.3 1.3 convert_element_type.135
  15.6 0.8 convert_element_type.137
  16.4 0.1 fusion.29
  16.5 2.7 pad_maximum_fusion.1
  19.2 10.7 %all-to-all-done = bf16[32,2,64,128]{3,2,1,0:T(8,128)(2,1)S(1)} async-done(((bf16[32,2,64,128]{3,2,1,0:T(8,128)(2,1)}), bf16[32,2,64,128]{3,2,1,0:T(8,128)(2,1)S(1)}, u32[]{:S(2)}, u32[]{:S(2)}) %all-to-all-start) | async-done | bytes 1048608 | tf_op jit(solution)/shard_map/all_to_all | solution.py:480
  29.9 1.0 copy-done.2
  30.9 4.1 %all-to-all-start.1 = ((bf16[32,4,64,128]{3,2,1,0:T(8,128)(2,1)}), bf16[32,4,64,128]{3,2,1,0:T(8,128)(2,1)S(1)}, u32[]{:S(2)}, u32[]{:S(2)}) async-start(bf16[32,4,64,128]{3,2,1,0:T(8,128)(2,1)} %pad_maximum_fusion.1), calls=%async_computation.1 | async-start | bytes 4194304 | tf_op jit(solution)/shard_map/all_to_all | solution.py:480
  35.0 0.6 fusion.43
  35.6 0.1 convert_reduce_fusion
  35.7 0.1 select_reduce_fusion.3
  35.8 1.3 fusion.45
  37.1 0.1 select_reduce_fusion
  37.2 0.8 constant_dynamic-slice_fusion
  38.1 1.2 copy-done.3
  39.3 1.0 shard_map.154
  40.3 174.1 %shard_map.155 = (bf16[3,11,2,4,4,4,64,128]{7,6,5,4,3,2,1,0:T(8,128)(2,1)}, bf16[32,8,2048]{2,1,0:T(8,128)(2,1)S(1)}, bf16[32,8,1024]{2,1,0:T(8,128)(2,1)S(1)}, ...) custom-call(s32[16]{0:T(128)S(1)} %compare_convert_fusion.1.refs_0_.twice_ref, bf16[3,11,64,128]{3,2,1,0:T(8,128)(2,1)S(1)} %bitcast.63, ...), custom_call_target="tpu_custom_call" | custom-call | flops 1073741824 | bytes 419430400 | tf_op jit(solution)/shard_map/pallas_call | solution.py:280
  214.4 1.0 copy-done.4
  215.4 0.8 copy-done.6
  216.2 1.1 shard_map.156
  217.3 1.3 copy-done.1
  218.7 5.9 %all-to-all-start.2 = ((bf16[32,4,64,128]{3,2,1,0:T(8,128)(2,1)}), bf16[32,4,64,128]{3,2,1,0:T(8,128)(2,1)}, u32[]{:S(2)}, u32[]{:S(2)}) async-start(bf16[32,4,64,128]{3,2,1,0:T(8,128)(2,1)} %bitcast.61), calls=%async_computation.2 | async-start | bytes 4194304 | tf_op jit(solution)/shard_map/all_to_all | solution.py:480
  224.6 1.8 fusion.16
  226.4 1.1 copy.38
  227.4 0.3 fusion.20
  227.8 0.3 copy.43
  228.1 29.2 %shard_map.157 = (bf16[24,8,1024]{2,1,0:T(8,128)(2,1)S(1)}, bf16[24,8,512]{2,1,0:T(8,128)(2,1)S(1)}) custom-call(s32[16]{0:T(128)S(1)} %compare_convert_fusion.1.refs_0_.twice_ref, f32[8,2048]{1,0:T(8,128)S(1)} %pad_convert_fusion.g_ref, bf16[3,11,32,4,64,128]{5,4,3,2,1,0:T(8,128)(2,1)} %bitcast.8.weight_ref, bf16[32,8,2048]{2,1,0:T(8,128)(2,1)S(1)} %copy-done.5, ...), custom_call_target="tpu_custom_call" | custom-call | flops 1073741824 | bytes 134217728 | tf_op jit(solution)/shard_map/pallas_call | solution.py:383
  257.3 0.5 fusion.18
  257.8 0.3 copy.41
  258.1 0.3 fusion.22
  258.5 0.3 copy.44
  258.8 1.3 broadcast_in_dim.130
  260.1 0.3 broadcast_in_dim.131
  260.4 2.5 pad_maximum_fusion
  262.9 8.5 %all-to-all-start.3 = ((bf16[128,8,2304]{2,1,0:T(8,128)(2,1)}), bf16[128,8,2304]{2,1,0:T(8,128)(2,1)}, u32[]{:S(2)}, u32[]{:S(2)}) async-start(bf16[128,8,2304]{2,1,0:T(8,128)(2,1)} %bitcast.64), calls=%async_computation.3 | async-start | bytes 9437184 | tf_op jit(solution)/shard_map/all_to_all | solution.py:531
  272.2 0.6 compare_reduce_fusion
  272.8 2.1 constant_dynamic-slice_fusion.3
  274.9 2.1 convert_element_type.139
  276.9 2.0 slice_multiply_fusion
  278.9 51.0 %all-to-all-done.3 = bf16[128,8,2304]{2,1,0:T(8,128)(2,1)} async-done(((bf16[128,8,2304]{2,1,0:T(8,128)(2,1)}), bf16[128,8,2304]{2,1,0:T(8,128)(2,1)}, u32[]{:S(2)}, u32[]{:S(2)}) %all-to-all-start.3) | async-done | bytes 4718624 | tf_op jit(solution)/shard_map/all_to_all | solution.py:531
  329.9 1.2 broadcast_select_fusion.1
  331.2 2.3 fusion.2
  333.6 2.5 fusion
  336.3 3.8 %fusion.7 = (bf16[1,2048,128]{2,1,0:T(8,128)(2,1)}, f32[1,2048,128]{2,1,0:T(8,128)}, f32[1,2048,128]{2,1,0:T(8,128)}, bf16[1,2048,128]{2,1,0:T(8,128)(2,1)}, f32...) fusion(bf16[1,1,32,1,64,128]{5,4,3,2,1,0:T(8,128)(2,1)S(1)} %get-tuple-element.46, pred[]{:T(512)} %compare_reduce_fusion, ...), kind=kLoop, calls=%fused_computation.19 | loop fusion | flops 6815744 | bytes 12582913 | tf_op jit(solution)/shard_map/convert_element_type | solution.py:442
  (44 shorter events, 0.6 us)
Async XLA Ops:
  0.6 36.6 %copy-start = (bf16[128,2048]{1,0:T(8,128)(2,1)S(1)}, bf16[128,2048]{1,0:T(8,128)(2,1)}, u32[]{:S(2)}) copy-start(bf16[128,2048]{1,0:T(8,128)(2,1)} %param.11) | copy-start | bytes 1572868
  0.6 12.2 %copy-start.10 = (f32[1,2048,128]{2,1,0:T(8,128)S(1)}, f32[1,2048,128]{2,1,0:T(8,128)}, u32[]{:S(2)}) copy-start(f32[1,2048,128]{2,1,0:T(8,128)} %param.15) | copy-start | bytes 3145732
  4.0 12.4 %copy-start.13 = (s32[24]{0:T(128)S(1)}, s32[24]{0:T(128)}, u32[]{:S(2)}) copy-start(s32[24]{0:T(128)} %param.21) | copy-start | bytes 292
  4.0 25.9 %all-to-all-start = ((bf16[32,2,64,128]{3,2,1,0:T(8,128)(2,1)}), bf16[32,2,64,128]{3,2,1,0:T(8,128)(2,1)S(1)}, u32[]{:S(2)}, u32[]{:S(2)}) async-start(bf16[32,2,64,128]{3,2,1,0:T(8,128)(2,1)} %pad_maximum_fusion.2), calls=%async_computation | async-start | bytes 2097152 | tf_op jit(solution)/shard_map/all_to_all | solution.py:480
  12.9 2.7 copy-start.11
  15.6 20.0 %copy-start.12 = (s32[24]{0:T(128)S(1)}, s32[24]{0:T(128)}, u32[]{:S(2)}) copy-start(s32[24]{0:T(128)} %param.19) | copy-start | bytes 292
  15.6 20.0 %copy-start.14 = (s32[16]{0:T(128)S(1)}, s32[16]{0:T(128)}, u32[]{:S(2)}) copy-start(s32[16]{0:T(128)} %param.20) | copy-start | bytes 196
  29.9 1.0 copy-start.2
  30.9 185.3 %all-to-all-start.1 = ((bf16[32,4,64,128]{3,2,1,0:T(8,128)(2,1)}), bf16[32,4,64,128]{3,2,1,0:T(8,128)(2,1)S(1)}, u32[]{:S(2)}, u32[]{:S(2)}) async-start(bf16[32,4,64,128]{3,2,1,0:T(8,128)(2,1)} %pad_maximum_fusion.1), calls=%async_computation.1 | async-start | bytes 4194304 | tf_op jit(solution)/shard_map/all_to_all | solution.py:480
  38.1 1.2 copy-start.3
  214.4 1.0 copy-start.4
  215.4 0.8 copy-start.6
  217.3 1.4 copy-start.1
  218.7 9.5 %copy-start.5 = (bf16[32,8,2048]{2,1,0:T(8,128)(2,1)S(1)}, bf16[32,8,2048]{2,1,0:T(8,128)(2,1)}, u32[]{:S(2)}) copy-start(bf16[32,8,2048]{2,1,0:T(8,128)(2,1)} %copy-done.4) | copy-start | bytes 3145732
  218.7 44.2 %all-to-all-start.2 = ((bf16[32,4,64,128]{3,2,1,0:T(8,128)(2,1)}), bf16[32,4,64,128]{3,2,1,0:T(8,128)(2,1)}, u32[]{:S(2)}, u32[]{:S(2)}) async-start(bf16[32,4,64,128]{3,2,1,0:T(8,128)(2,1)} %bitcast.61), calls=%async_computation.2 | async-start | bytes 4194304 | tf_op jit(solution)/shard_map/all_to_all | solution.py:480
  262.9 67.1 %all-to-all-start.3 = ((bf16[128,8,2304]{2,1,0:T(8,128)(2,1)}), bf16[128,8,2304]{2,1,0:T(8,128)(2,1)}, u32[]{:S(2)}, u32[]{:S(2)}) async-start(bf16[128,8,2304]{2,1,0:T(8,128)(2,1)} %bitcast.64), calls=%async_computation.3 | async-start | bytes 9437184 | tf_op jit(solution)/shard_map/all_to_all | solution.py:531
  333.6 2.6 copy-start.7
  333.6 2.6 copy-start.8
  333.6 2.6 copy-start.9
